TPU v7x, 256 devices: a whole 4x4x8 slice. The times are simulated.
256 devices in a mesh: section: 16 (over z, core), expert: 16 (over x, y).
Axes of the slice: x: 4, y: 4, z: 8, core: 2. Of those that a mesh axis runs over, the one named last changes fastest.
Arguments:
- forward_in: bfloat16 [16, 1024, 3584], P('section', 'expert'), may hold values from -20 to 20
- reverse_in: bfloat16 [16, 1024, 3584], P('section', 'expert'), may hold values from -20 to 20
- w_gate: bfloat16 [16, 3584, 8192], P('section', None, 'expert'), may hold values from -0.09375 to 0.09375
- w_up: bfloat16 [16, 3584, 8192], P('section', None, 'expert'), may hold values from -0.09375 to 0.09375
- w_down: bfloat16 [16, 8192, 3584], P('section', 'expert'), may hold values from -0.1875 to 0.1875
- routes: int32 [16, 2, 16, 1024, 1], P('section', None, None, 'expert'), may hold values from 0 to 7; in each aligned block of 64 rows (0 to 63, 64 to 127, ..., all dimensions but the last counted through in order) at most 24 rows name the same one
- gate_weight: float32 [16, 2, 16, 1024], P('section', None, None, 'expert'), may hold values from 0.5 to 1.5
Outputs:
- forward_out: bfloat16 [16, 1024, 3584], P('section', 'expert')
- reverse_out: bfloat16 [16, 1024, 3584], P('section', 'expert')
Inputs may be any that keep to these rules, and one draw needn't show every extreme that they name: `routes`: within each block of 64 tokens of one layer, direction and micro-batch, no expert is chosen more than 24 times, and in some of these blocks one expert is chosen exactly 24 times.
All inputs are finite; a program needn't handle non-finite values.
Results may differ from a plain program's by a relative error of at most 0.0067.
Values may be sent and summed in bfloat16 or wider, within the bound.
No kernel may reach another device: no remote copies, remote signals or barrier semaphores. Data moves between devices by JAX's collectives and lax.ppermute only.
A program may use at most 128 MiB of HBM per device.

v0:
```python
import jax
import jax.numpy as jnp
from jax import lax
from jax.sharding import PartitionSpec as P

epsilon = 1e-06


def passed_along(array, axis, by):
    length = lax.axis_size(axis)
    return lax.ppermute(array, axis, [(i, (i + by) % length) for i in range(length)])


def normalize(token_rows):
    widened = token_rows.astype(jnp.float32)
    inverse = lax.rsqrt(jnp.mean(widened * widened, axis=-1, keepdims=True) + epsilon)
    return (widened * inverse).astype(jnp.bfloat16)


def slot_plan(chosen, experts, capacity, offset):
    onehot = (chosen[:, None] == jnp.arange(experts, dtype=jnp.int32)[None, :]).astype(jnp.int32)
    ranked = jnp.sum((jnp.cumsum(onehot, axis=0) - onehot) * onehot, axis=1)
    return chosen * capacity + offset + ranked


def pack_rows(slot_of, normed, slot_total):
    select = (jnp.arange(slot_total, dtype=jnp.int32)[:, None] == slot_of[None, :]).astype(
        jnp.bfloat16
    )
    return jnp.dot(select, normed, preferred_element_type=jnp.float32).astype(jnp.bfloat16)


def expert_part(received, gate_cols, up_cols, down_rows):
    features = received.shape[-1]
    flattened = received.reshape(-1, features)
    gate_out = jnp.dot(flattened, gate_cols, preferred_element_type=jnp.float32)
    up_out = jnp.dot(flattened, up_cols, preferred_element_type=jnp.float32)
    active = (jax.nn.silu(gate_out) * up_out).astype(jnp.bfloat16)
    partial_value = jnp.dot(active, down_rows, preferred_element_type=jnp.float32).astype(
        jnp.bfloat16
    )
    return partial_value.reshape(received.shape)


def expert_layer(packed, gate_cols, up_cols, down_rows):
    experts, capacity, features = packed.shape
    outgoing = jnp.repeat(packed, 2, axis=0)
    partials = expert_part(
        lax.all_to_all(outgoing, "expert", split_axis=0, concat_axis=0, tiled=True),
        gate_cols,
        up_cols,
        down_rows,
    )
    returned = lax.all_to_all(partials, "expert", split_axis=0, concat_axis=0, tiled=True)
    return (
        returned.reshape(experts, 2, capacity, features)
        .astype(jnp.float32)
        .sum(axis=1)
        .astype(jnp.bfloat16)
    )


def local(forward_in, reverse_in, w_gate, w_up, w_down, routes, gate_weight):
    sections = lax.axis_size("section")
    tick_count = min(2, sections - 1)
    devices = lax.axis_size("expert")
    experts = devices // 2
    token_count = forward_in.shape[1]
    features = forward_in.shape[2]
    most_rows = min(token_count, 3 * token_count // experts)
    position = lax.axis_index("section")
    gate_cols = w_gate[0]
    up_cols = w_up[0]
    down_rows = w_down[0]
    forward_routes = routes[0, 0, :, :, 0]
    reverse_routes = routes[0, 1, :, :, 0]
    forward_gates = gate_weight[0, 0]
    reverse_gates = gate_weight[0, 1]

    def advance(tick_index, carried):
        forward_x, reverse_x = carried
        forward_batch = (position - tick_index) % sections
        reverse_batch = (position + tick_index) % sections
        forward_live = tick_index <= position
        reverse_live = position + tick_index < sections
        forward_ids = lax.dynamic_index_in_dim(forward_routes, forward_batch, 0, keepdims=False)
        reverse_ids = lax.dynamic_index_in_dim(reverse_routes, reverse_batch, 0, keepdims=False)
        forward_scale = lax.dynamic_index_in_dim(forward_gates, forward_batch, 0, keepdims=False)
        reverse_scale = lax.dynamic_index_in_dim(reverse_gates, reverse_batch, 0, keepdims=False)
        forward_normed = normalize(forward_x)
        reverse_normed = normalize(reverse_x)
        slot_span = 2 * most_rows
        forward_slots = slot_plan(forward_ids, experts, slot_span, 0)
        reverse_slots = slot_plan(reverse_ids, experts, slot_span, most_rows)
        packed = pack_rows(
            jnp.concatenate([forward_slots, reverse_slots]),
            jnp.concatenate([forward_normed, reverse_normed], axis=0),
            experts * slot_span,
        )
        merged = expert_layer(
            packed.reshape(experts, slot_span, features), gate_cols, up_cols, down_rows
        )
        flat_out = merged.reshape(experts * slot_span, features)
        forward_y = jnp.take(flat_out, forward_slots, axis=0)
        reverse_y = jnp.take(flat_out, reverse_slots, axis=0)
        forward_new = (
            forward_x.astype(jnp.float32) + forward_scale[:, None] * forward_y.astype(jnp.float32)
        ).astype(jnp.bfloat16)
        reverse_new = (
            reverse_x.astype(jnp.float32) + reverse_scale[:, None] * reverse_y.astype(jnp.float32)
        ).astype(jnp.bfloat16)
        forward_x = jnp.where(forward_live, forward_new, forward_x)
        reverse_x = jnp.where(reverse_live, reverse_new, reverse_x)
        forward_x = passed_along(forward_x, "section", 1)
        reverse_x = passed_along(reverse_x, "section", -1)
        return (forward_x, reverse_x)

    finished = lax.fori_loop(0, tick_count, advance, (forward_in[0], reverse_in[0]))
    return (finished[0][None], finished[1][None])


def solution(mesh):
    return jax.shard_map(
        local,
        mesh=mesh,
        in_specs=(
            P("section", "expert", None),
            P("section", "expert", None),
            P("section", None, "expert"),
            P("section", None, "expert"),
            P("section", "expert", None),
            P("section", None, None, "expert", None),
            P("section", None, None, "expert"),
        ),
        out_specs=(P("section", "expert", None), P("section", "expert", None)),
        check_vma=False,
    )
```

profile of v0, /device:TPU:73, one launch (start us, length us, event | category | flops | bytes accessed | tf_op | source)
XLA Modules:
  0.0 401.7 jit_solution(18254821256098836299)
XLA Ops:
  0.6 1.0 copy.24
  1.6 1.8 copy.25
  3.5 0.7 slice_bitcast_fusion.2
  4.2 0.7 slice_bitcast_fusion
  4.9 394.2 %while.17 = (s32[]{:T(128)}, bf16[64,3584]{1,0:T(8,128)(2,1)S(1)}, bf16[64,3584]{1,0:T(8,128)(2,1)}, s32[]{:T(128)}, f32[16,64]{1,0:T(8,128)S(1)}, /*index=5*/s3...) while((s32[]{:T(128)}, bf16[64,3584]{1,0:T(8,128)(2,1)S(1)}, ...), condition=%wide.region_8.10_spmd, body=%wide.region_0.9_spmd.sunk | while | flops 8823825408 | bytes 126128016 | solution.py:118
  5.1 0.2 select_reduce_fusion.5
  5.5 0.2 select_reduce_fusion.4
  5.7 1.3 fusion.49
  7.0 1.2 fusion.50
  8.2 0.1 fusion.51
  8.4 0.9 convolution_convert_fusion.4
  9.3 0.5 broadcast_in_dim.75
  9.8 69.3 %all_to_all.26 = bf16[16,48,3584]{2,1,0:T(8,128)(2,1)S(1)} all-to-all(bf16[16,48,3584]{2,1,0:T(8,128)(2,1)S(1)} %bitcast.67), channel_id=1, replica_groups=mesh['section'=16,'expert'=16] {'expert'}, dimensions={0} | all-to-all | bytes 11010048 | tf_op jit(solution)/shard_map/while/body/eval_jaxpr/all_to_all | solution.py:49
  79.1 3.0 fusion.55
  82.1 13.1 %convolution_convert_fusion.5 = bf16[768,3584]{1,0:T(8,128)(2,1)} fusion(bf16[512,3584]{1,0:T(8,128)(2,1)} %get-tuple-element.428, f32[768,512]{1,0:T(8,128)S(1)} %fusion.55, bf16[768,3584]{1,0:T(8,128)(2,1)} %bitcast.71, bf16[3584,512]{1,0:T(8,128)(2,1)} %get-tuple-element.427), kind=kOutput, calls=%fused_computation.2.clone.1 | convolution fusion | flops 5642256384 | bytes 19922944 | tf_op jit(solution)/shard_map/while/body/eval_jaxpr/dot_general | solution.py:39
  95.2 6.1 %all-to-all-start.1 = ((bf16[16,48,3584]{2,1,0:T(8,128)(2,1)}), bf16[16,48,3584]{2,1,0:T(8,128)(2,1)}, u32[]{:S(2)}, u32[]{:S(2)}) async-start(bf16[16,48,3584]{2,1,0:T(8,128)(2,1)} %bitcast.69), calls=%async_computation.1 | async-start | bytes 11010048 | tf_op jit(solution)/shard_map/while/body/eval_jaxpr/all_to_all | solution.py:54
  101.3 66.1 %all-to-all-done.1 = bf16[16,48,3584]{2,1,0:T(8,128)(2,1)} async-done(((bf16[16,48,3584]{2,1,0:T(8,128)(2,1)}), bf16[16,48,3584]{2,1,0:T(8,128)(2,1)}, u32[]{:S(2)}, u32[]{:S(2)}) %all-to-all-start.1) | async-done | bytes 5505056 | tf_op jit(solution)/shard_map/while/body/eval_jaxpr/all_to_all | solution.py:54
  167.4 3.8 bitcast_reduce_fusion.2
  171.3 1.6 gather_fusion.1
  172.9 2.4 fusion.59
  175.2 4.7 %collective-permute-start.1 = (bf16[64,3584]{1,0:T(8,128)(2,1)}, bf16[64,3584]{1,0:T(8,128)(2,1)}, u32[]{:S(2)}, u32[]{:S(2)}) collective-permute-start(bf16[64,3584]{1,0:T(8,128)(2,1)} %fusion.59), channel_id=1, source_target_pairs={{0,240},{16,0},{32,16},{48,32},{64,48},{80,64},{96,80},{112,96},{1... | collective-permute-start | bytes 1376264 | tf_op jit(solution)/shard_map/while/body/eval_jaxpr/ppermute | solution.py:11
  179.9 1.6 gather_fusion
  181.5 1.3 fusion.57
  182.8 1.5 collective-permute-start
  184.4 3.8 collective-permute-done.1
  188.1 1.7 collective-permute-done
  190.0 0.2 select_reduce_fusion.5
  190.3 0.2 select_reduce_fusion.4
  190.5 1.3 fusion.49
  191.9 1.2 fusion.50
  193.3 0.9 convolution_convert_fusion.4
  194.1 0.5 broadcast_in_dim.75
  194.7 78.1 %all_to_all.26 = bf16[16,48,3584]{2,1,0:T(8,128)(2,1)S(1)} all-to-all(bf16[16,48,3584]{2,1,0:T(8,128)(2,1)S(1)} %bitcast.67), channel_id=1, replica_groups=mesh['section'=16,'expert'=16] {'expert'}, dimensions={0} | all-to-all | bytes 11010048 | tf_op jit(solution)/shard_map/while/body/eval_jaxpr/all_to_all | solution.py:49
  272.8 3.0 fusion.55
  275.8 13.1 %convolution_convert_fusion.5 = bf16[768,3584]{1,0:T(8,128)(2,1)} fusion(bf16[512,3584]{1,0:T(8,128)(2,1)} %get-tuple-element.428, f32[768,512]{1,0:T(8,128)S(1)} %fusion.55, bf16[768,3584]{1,0:T(8,128)(2,1)} %bitcast.71, bf16[3584,512]{1,0:T(8,128)(2,1)} %get-tuple-element.427), kind=kOutput, calls=%fused_computation.2.clone.1 | convolution fusion | flops 5642256384 | bytes 19922944 | tf_op jit(solution)/shard_map/while/body/eval_jaxpr/dot_general | solution.py:39
  288.9 6.3 %all-to-all-start.1 = ((bf16[16,48,3584]{2,1,0:T(8,128)(2,1)}), bf16[16,48,3584]{2,1,0:T(8,128)(2,1)}, u32[]{:S(2)}, u32[]{:S(2)}) async-start(bf16[16,48,3584]{2,1,0:T(8,128)(2,1)} %bitcast.69), calls=%async_computation.1 | async-start | bytes 11010048 | tf_op jit(solution)/shard_map/while/body/eval_jaxpr/all_to_all | solution.py:54
  295.2 65.8 %all-to-all-done.1 = bf16[16,48,3584]{2,1,0:T(8,128)(2,1)} async-done(((bf16[16,48,3584]{2,1,0:T(8,128)(2,1)}), bf16[16,48,3584]{2,1,0:T(8,128)(2,1)}, u32[]{:S(2)}, u32[]{:S(2)}) %all-to-all-start.1) | async-done | bytes 5505056 | tf_op jit(solution)/shard_map/while/body/eval_jaxpr/all_to_all | solution.py:54
  361.0 3.8 bitcast_reduce_fusion.2
  364.8 1.6 gather_fusion.1
  366.4 2.4 fusion.59
  368.8 4.9 %collective-permute-start.1 = (bf16[64,3584]{1,0:T(8,128)(2,1)}, bf16[64,3584]{1,0:T(8,128)(2,1)}, u32[]{:S(2)}, u32[]{:S(2)}) collective-permute-start(bf16[64,3584]{1,0:T(8,128)(2,1)} %fusion.59), channel_id=1, source_target_pairs={{0,240},{16,0},{32,16},{48,32},{64,48},{80,64},{96,80},{112,96},{1... | collective-permute-start | bytes 1376264 | tf_op jit(solution)/shard_map/while/body/eval_jaxpr/ppermute | solution.py:11
  373.7 1.6 gather_fusion
  375.3 1.3 fusion.57
  376.6 17.1 %collective-permute-start = (bf16[64,3584]{1,0:T(8,128)(2,1)S(1)}, bf16[64,3584]{1,0:T(8,128)(2,1)S(1)}, u32[]{:S(2)}, u32[]{:S(2)}) collective-permute-start(bf16[64,3584]{1,0:T(8,128)(2,1)S(1)} %fusion.57), channel_id=1, source_target_pairs={{0,16},{16,32},{32,48},{48,64},{64,80},{80,96},{96,112},{112,128},... | collective-permute-start | bytes 1376264 | tf_op jit(solution)/shard_map/while/body/eval_jaxpr/ppermute | solution.py:11
  393.7 3.6 collective-permute-done.1
  397.2 1.9 collective-permute-done
  399.1 0.8 copy.26
  399.9 1.8 copy.27
  (41 shorter events, 1.2 us)
Async XLA Ops:
  9.8 69.3 %copy-start.1 = (bf16[3584,512]{1,0:T(8,128)(2,1)S(1)}, bf16[3584,512]{1,0:T(8,128)(2,1)}, u32[]{:S(2)}) copy-start(bf16[3584,512]{1,0:T(8,128)(2,1)} %get-tuple-element.426) | copy-start | bytes 11010052 | tf_op jit(solution)/shard_map/while
  79.1 3.0 copy-start
  95.2 72.3 %all-to-all-start.1 = ((bf16[16,48,3584]{2,1,0:T(8,128)(2,1)}), bf16[16,48,3584]{2,1,0:T(8,128)(2,1)}, u32[]{:S(2)}, u32[]{:S(2)}) async-start(bf16[16,48,3584]{2,1,0:T(8,128)(2,1)} %bitcast.69), calls=%async_computation.1 | async-start | bytes 11010048 | tf_op jit(solution)/shard_map/while/body/eval_jaxpr/all_to_all | solution.py:54
  175.2 12.9 %collective-permute-start.1 = (bf16[64,3584]{1,0:T(8,128)(2,1)}, bf16[64,3584]{1,0:T(8,128)(2,1)}, u32[]{:S(2)}, u32[]{:S(2)}) collective-permute-start(bf16[64,3584]{1,0:T(8,128)(2,1)} %fusion.59), channel_id=1, source_target_pairs={{0,240},{16,0},{32,16},{48,32},{64,48},{80,64},{96,80},{112,96},{1... | collective-permute-start | bytes 1376264 | tf_op jit(solution)/shard_map/while/body/eval_jaxpr/ppermute | solution.py:11
  182.8 7.0 %collective-permute-start = (bf16[64,3584]{1,0:T(8,128)(2,1)S(1)}, bf16[64,3584]{1,0:T(8,128)(2,1)S(1)}, u32[]{:S(2)}, u32[]{:S(2)}) collective-permute-start(bf16[64,3584]{1,0:T(8,128)(2,1)S(1)} %fusion.57), channel_id=1, source_target_pairs={{0,16},{16,32},{32,48},{48,64},{64,80},{80,96},{96,112},{112,128},... | collective-permute-start | bytes 1376264 | tf_op jit(solution)/shard_map/while/body/eval_jaxpr/ppermute | solution.py:11
  194.7 78.1 %copy-start.1 = (bf16[3584,512]{1,0:T(8,128)(2,1)S(1)}, bf16[3584,512]{1,0:T(8,128)(2,1)}, u32[]{:S(2)}) copy-start(bf16[3584,512]{1,0:T(8,128)(2,1)} %get-tuple-element.426) | copy-start | bytes 11010052 | tf_op jit(solution)/shard_map/while
  272.8 3.0 copy-start
  288.9 72.1 %all-to-all-start.1 = ((bf16[16,48,3584]{2,1,0:T(8,128)(2,1)}), bf16[16,48,3584]{2,1,0:T(8,128)(2,1)}, u32[]{:S(2)}, u32[]{:S(2)}) async-start(bf16[16,48,3584]{2,1,0:T(8,128)(2,1)} %bitcast.69), calls=%async_computation.1 | async-start | bytes 11010048 | tf_op jit(solution)/shard_map/while/body/eval_jaxpr/all_to_all | solution.py:54
  368.8 28.5 %collective-permute-start.1 = (bf16[64,3584]{1,0:T(8,128)(2,1)}, bf16[64,3584]{1,0:T(8,128)(2,1)}, u32[]{:S(2)}, u32[]{:S(2)}) collective-permute-start(bf16[64,3584]{1,0:T(8,128)(2,1)} %fusion.59), channel_id=1, source_target_pairs={{0,240},{16,0},{32,16},{48,32},{64,48},{80,64},{96,80},{112,96},{1... | collective-permute-start | bytes 1376264 | tf_op jit(solution)/shard_map/while/body/eval_jaxpr/ppermute | solution.py:11
  376.6 22.5 %collective-permute-start = (bf16[64,3584]{1,0:T(8,128)(2,1)S(1)}, bf16[64,3584]{1,0:T(8,128)(2,1)S(1)}, u32[]{:S(2)}, u32[]{:S(2)}) collective-permute-start(bf16[64,3584]{1,0:T(8,128)(2,1)S(1)} %fusion.57), channel_id=1, source_target_pairs={{0,16},{16,32},{32,48},{48,64},{64,80},{80,96},{96,112},{112,128},... | collective-permute-start | bytes 1376264 | tf_op jit(solution)/shard_map/while/body/eval_jaxpr/ppermute | solution.py:11
where the time goes:
time: 408 us; the launch traced here: 402 us
  blocking collectives  147 us (36%)
  waiting for transfers between devices  143 us (35%)
  starting transfers between devices  40.6 us (10%)
  matrix products  33.8 us (8%)
  other arithmetic  21.9 us (5%)
  local copies, waits for them, and re-layouts  14.4 us (4%)
    all_to_all x2, blocking collectives, expert_layer(): lax.all_to_all(outgoing, 'expert', split_axis=0, concat_axis=0, tiled=True)  147 us
    all_to_all x2, waiting for transfers between devices, expert_layer(): lax.all_to_all(partials, 'expert', split_axis=0, concat_axis=0, tiled=True)  132 us
    ppermute x4, starting transfers between devices, passed_along(): lax.ppermute(array, axis, [(i, (i + by) % length) for i in range(length)])  28.3 us
    dot_general x2, matrix products, expert_part(): jnp.dot(active, down_rows, preferred_element_type=jnp.float32)  26.2 us
    all_to_all x2, starting transfers between devices, expert_layer(): lax.all_to_all(partials, 'expert', split_axis=0, concat_axis=0, tiled=True)  12.4 us
    ppermute x4, waiting for transfers between devices, passed_along(): lax.ppermute(array, axis, [(i, (i + by) % length) for i in range(length)])  10.8 us
  transfers between devices with their start and end apart: 6, of which 6 were waited for; matrix products, arithmetic and copies ran while one was open for 1% of the time, Pallas kernels for 0%

commit v1 on v0

v1 whole, which is shorter than its diff:
```python
import jax
import jax.numpy as jnp
from jax import lax
from jax.experimental import pallas as pl
from jax.experimental.pallas import tpu as pltpu
from jax.sharding import PartitionSpec as P

epsilon = 1e-06
MIB = 1 << 20


def together(*arrays):
    return lax.optimization_barrier(arrays)


def bits(mask):
    return mask.astype(jnp.float32).astype(jnp.bfloat16)


def normed_select(slots, parts, slot_total):
    widened = [part.astype(jnp.float32) for part in parts]
    total = sum(jnp.sum(part * part, axis=-1, keepdims=True) for part in widened)
    width = sum(part.shape[1] for part in parts)
    inverse = lax.rsqrt(total / width + epsilon)
    select = bits(lax.broadcasted_iota(jnp.int32, (slot_total, slots.shape[1]), 0) == slots)
    packed = []
    for part in widened:
        normed = (part * inverse).astype(jnp.bfloat16)
        rows = jnp.dot(select, normed, preferred_element_type=jnp.float32)
        packed.append(rows.astype(jnp.bfloat16))
    return packed


def first_pack_kernel(slots_ref, own_ref, mate_ref, out_ref):
    rows = jnp.concatenate([own_ref[...], mate_ref[...]], axis=0)
    out_ref[...] = normed_select(slots_ref[...], [rows], out_ref.shape[0])[0]


def pack_kernel(group_ref, slots_ref, near_ref, far_ref, out_ref):
    near, far = near_ref[...], far_ref[...]
    half = near.shape[1]
    count = far.shape[0] // 2
    far = jnp.concatenate([far[count:], far[:count]], axis=0)
    first = group_ref[...] == 0
    parts = [jnp.where(first, near, far), jnp.where(first, far, near)]
    low, high = normed_select(slots_ref[...], parts, out_ref.shape[0])
    out_ref[:, :half] = low
    out_ref[:, half:] = high


def pack(kernel, slot_total, features, *operands):
    rows = 128
    return pl.pallas_call(
        kernel,
        out_shape=jax.ShapeDtypeStruct((slot_total, features), jnp.bfloat16),
        compiler_params=pltpu.CompilerParams(vmem_limit_bytes=32 * MIB),
        cost_estimate=pl.CostEstimate(
            flops=2 * slot_total * rows * features,
            bytes_accessed=2 * (slot_total + rows) * features,
            transcendentals=0,
        ),
    )(*operands)


def hidden_kernel(rows_ref, gate_ref, up_ref, out_ref):
    rows = rows_ref[...]
    gate_out = jnp.dot(rows, gate_ref[...], preferred_element_type=jnp.float32)
    up_out = jnp.dot(rows, up_ref[...], preferred_element_type=jnp.float32)
    out_ref[...] = (gate_out / (1.0 + jnp.exp(-gate_out)) * up_out).astype(jnp.bfloat16)


def hidden(rows, gate_cols, up_cols):
    count, features = rows.shape
    width = gate_cols.shape[1]
    block = min(256, width)
    return pl.pallas_call(
        hidden_kernel,
        grid=(width // block,),
        in_specs=[
            pl.BlockSpec((count, features), lambda j: (0, 0)),
            pl.BlockSpec((features, block), lambda j: (0, j)),
            pl.BlockSpec((features, block), lambda j: (0, j)),
        ],
        out_specs=pl.BlockSpec((count, block), lambda j: (0, j)),
        out_shape=jax.ShapeDtypeStruct((count, width), jnp.bfloat16),
        compiler_params=pltpu.CompilerParams(vmem_limit_bytes=32 * MIB),
        cost_estimate=pl.CostEstimate(
            flops=4 * count * features * width,
            bytes_accessed=2 * (count * features + 2 * features * width + count * width),
            transcendentals=count * width,
        ),
    )(rows, gate_cols, up_cols)


def down_kernel(own_ref, mate_ref, own_rows_ref, *refs):
    mate_rows_refs, out_ref = refs[:-1], refs[-1]
    total = jnp.dot(own_ref[...], own_rows_ref[...], preferred_element_type=jnp.float32)
    start = 0
    for rows_ref in mate_rows_refs:
        stop = start + rows_ref.shape[0]
        total = total + jnp.dot(
            mate_ref[:, start:stop], rows_ref[...], preferred_element_type=jnp.float32
        )
        start = stop
    out_ref[...] = total.astype(jnp.bfloat16)


def down(own, mate, own_rows, mate_rows):
    count, depth = own.shape
    width = own_rows.shape[1]
    block = width // 2
    whole = pl.BlockSpec((count, depth), lambda j: (0, 0))
    return pl.pallas_call(
        down_kernel,
        grid=(width // block,),
        in_specs=[whole, whole]
        + [pl.BlockSpec((rows.shape[0], block), lambda j: (0, j)) for rows in (own_rows, *mate_rows)],
        out_specs=pl.BlockSpec((count, block), lambda j: (0, j)),
        out_shape=jax.ShapeDtypeStruct((count, width), jnp.bfloat16),
        compiler_params=pltpu.CompilerParams(vmem_limit_bytes=32 * MIB),
        cost_estimate=pl.CostEstimate(
            flops=4 * count * depth * width,
            bytes_accessed=2 * (2 * count * depth + 2 * depth * width + count * width),
            transcendentals=0,
        ),
    )(own, mate, own_rows, *mate_rows)


def merge_kernel(live_ref, slots_ref, scale_ref, state_ref, returned_ref, out_ref):
    returned = returned_ref[...]
    shape = (state_ref.shape[0], returned.shape[0])
    select = bits(lax.broadcasted_iota(jnp.int32, shape, 1) == slots_ref[...])
    picked = jnp.dot(select, returned, preferred_element_type=jnp.float32)
    old = state_ref[...]
    new = (old.astype(jnp.float32) + scale_ref[...] * picked).astype(jnp.bfloat16)
    out_ref[...] = jnp.where(live_ref[...] > 0, new, old)


def merge(live, slots, scale, state, returned):
    rows, half = state.shape
    count = returned.shape[0]
    return pl.pallas_call(
        merge_kernel,
        out_shape=jax.ShapeDtypeStruct((rows, half), jnp.bfloat16),
        compiler_params=pltpu.CompilerParams(vmem_limit_bytes=32 * MIB),
        cost_estimate=pl.CostEstimate(
            flops=2 * rows * count * half,
            bytes_accessed=2 * (2 * rows + count) * half,
            transcendentals=0,
        ),
    )(live, slots.reshape(rows, 1), scale.reshape(rows, 1), state, returned)


def local(forward_in, reverse_in, w_gate, w_up, w_down, routes, gate_weight):
    sections = lax.axis_size("section")
    lanes = lax.axis_size("expert")
    tick_count = min(2, sections - 1)
    experts = lanes // 2
    token_count, features = forward_in.shape[1:]
    half = features // 2
    most_rows = min(token_count, 3 * token_count // experts)
    slot_total = lanes * most_rows
    position = lax.axis_index("section")
    lane = lax.axis_index("expert")
    side = lane % 2
    group = jnp.where((lane % 4 == 0) | (lane % 4 == 3), 0, 1)
    order = [0, 4, 3, 7, 1, 5, 2, 6]
    members = [2 * e if e % 2 == 0 else 2 * e + 1 for e in order]
    sides = [members, [i ^ 1 for i in members]]
    place = [order.index(e) for e in range(experts)]
    mates = [(i, i ^ 1) for i in range(lanes)]

    def to_mate(array):
        return lax.ppermute(array, "expert", mates)

    def to_section(array, direction, cross):
        by = -1 if direction else 1
        return lax.ppermute(
            array,
            ("section", "expert"),
            [
                (s * lanes + i, (s + by) % sections * lanes + (i ^ cross))
                for s in range(sections)
                for i in range(lanes)
            ],
        )

    def plan(direction, tick):
        batch = (position + (tick if direction else -tick)) % sections
        ids = lax.dynamic_index_in_dim(routes[0, direction, :, :, 0], batch, 0, keepdims=False)
        scale = lax.dynamic_index_in_dim(gate_weight[0, direction], batch, 0, keepdims=False)
        live = (position + tick < sections) if direction else (tick <= position)
        onehot = (ids[:, None] == jnp.arange(experts, dtype=jnp.int32)[None, :]).astype(jnp.int32)
        ranked = (jnp.cumsum(onehot, axis=0) - onehot) * onehot
        start = onehot * (jnp.array(place, jnp.int32) * (2 * most_rows))[None, :]
        return jnp.sum(ranked + start, axis=1), scale, live.astype(jnp.int32).reshape(1, 1)

    plans = [plan(direction, tick) for direction in range(2) for tick in range(tick_count)]
    own_plan = jnp.stack([p[0].astype(jnp.float32) for p in plans] + [p[1] for p in plans])
    mate_plan = to_mate(own_plan)
    own_slots = own_plan[: len(plans)].astype(jnp.int32) + side * most_rows
    mate_slots = mate_plan[: len(plans)].astype(jnp.int32) + (1 - side) * most_rows
    slots = jnp.concatenate([own_slots, mate_slots], axis=1)
    scales = jnp.concatenate([own_plan[len(plans) :], mate_plan[len(plans) :]], axis=1)
    group_flag = group.astype(jnp.int32).reshape(1, 1)

    def pair_slots(direction, tick):
        return slots[direction * tick_count + tick][None]

    gate_cols, up_cols, down_rows = w_gate[0], w_up[0], w_down[0]
    down_own = lax.dynamic_slice_in_dim(down_rows, group * half, half, 1)
    down_other = lax.dynamic_slice_in_dim(down_rows, (1 - group) * half, half, 1)
    depth = down_rows.shape[0] // 2

    def across(array):
        array = array.reshape(experts, 2 * most_rows, array.shape[-1])
        array = lax.all_to_all(array, "expert", 0, 0, axis_index_groups=sides, tiled=True)
        return array.reshape(slot_total, array.shape[-1])

    def expert(received, down_mate):
        active = hidden(received, gate_cols, up_cols)
        return down(active, to_mate(active), down_own, down_mate)

    def near_half(own, mate):
        at = group * half
        return jnp.concatenate(
            [lax.dynamic_slice_in_dim(rows, at, half, 1) for rows in (own, mate)], axis=0
        )

    def finish(direction, tick, near, returned):
        at = direction * tick_count + tick
        return merge(plans[at][2], slots[at], scales[at], near, returned)

    def repack(direction, tick, near, far):
        operands = (group_flag, pair_slots(direction, tick), near, far)
        return pack(pack_kernel, slot_total, features, *operands)

    def result(direction, near):
        own = to_section(near[:token_count], direction, 0)
        mate = to_section(near[token_count:], direction, 1)
        first = group == 0
        return jnp.concatenate(
            [jnp.where(first, own, mate), jnp.where(first, mate, own)], axis=1
        )[None]

    def first_pack(direction, own, mate):
        operands = (pair_slots(direction, 0), own, mate)
        return pack(first_pack_kernel, slot_total, features, *operands)

    forward, reverse = forward_in[0], reverse_in[0]
    forward_mate = to_mate(forward)
    packed_forward = first_pack(0, forward, forward_mate)
    reverse, packed_forward = together(reverse, packed_forward)
    reverse_mate = to_mate(reverse)
    reverse_mate, down_other = together(reverse_mate, down_other)
    down_mate = [to_mate(down_other[:depth])]
    for tick in range(tick_count):
        received = across(packed_forward)
        if tick:
            near = finish(1, tick - 1, reverse_near, returned_reverse)
            reverse_near, reverse_far = to_section(near, 1, 0), to_section(near, 1, 1)
            packed_reverse = repack(1, tick, reverse_near, reverse_far)
        else:
            packed_reverse = first_pack(1, reverse, reverse_mate)
            reverse_near = near_half(reverse, reverse_mate)
            forward_near = near_half(forward, forward_mate)
            packed_reverse, down_mate[0], down_other = together(
                packed_reverse, down_mate[0], down_other
            )
            down_mate.append(to_mate(down_other[depth:]))
        packed_reverse, received = together(packed_reverse, received)
        received_reverse = across(packed_reverse)
        out_forward = expert(received, down_mate)
        out_forward, received_reverse = together(out_forward, received_reverse)
        returned = across(out_forward)
        out_reverse = expert(received_reverse, down_mate)
        out_reverse, returned = together(out_reverse, returned)
        returned_reverse = across(out_reverse)
        near = finish(0, tick, forward_near, returned)
        if tick + 1 < tick_count:
            forward_near, forward_far = to_section(near, 0, 0), to_section(near, 0, 1)
            packed_forward = repack(0, tick + 1, forward_near, forward_far)
            packed_forward, returned_reverse = together(packed_forward, returned_reverse)
        else:
            forward_out = result(0, near)
    reverse_out = result(1, finish(1, tick, reverse_near, returned_reverse))
    return (forward_out, reverse_out)


def solution(mesh):
    return jax.shard_map(
        local,
        mesh=mesh,
        in_specs=(
            P("section", "expert", None),
            P("section", "expert", None),
            P("section", None, "expert"),
            P("section", None, "expert"),
            P("section", "expert", None),
            P("section", None, None, "expert", None),
            P("section", None, None, "expert"),
        ),
        out_specs=(P("section", "expert", None), P("section", "expert", None)),
        check_vma=False,
    )
```

time: 408 us -> 311 us (0.76); the launches traced: 402 us -> 309 us
  blocking collectives: 147 us -> 0 us
  Pallas kernels: 0 us -> 42.5 us
  starting transfers between devices: 40.6 us -> 80.3 us
  matrix products: 33.8 us -> 0 us
  local copies, waits for them, and re-layouts: 14.4 us -> 41.4 us
  other arithmetic: 21.9 us -> 4.44 us
    all_to_all x2 -> x0, blocking collectives: 147 us -> none  [expert_layer(): lax.all_to_all(outgoing, 'expert', split_axis=0, concat_axis=0, tiled=True)]
    all_to_all x2 -> x8, waiting for transfers between devices: 132 us -> 30.6 us  [across(): lax.all_to_all(array, 'expert', 0, 0, axis_index_groups=sides, tiled=True)]
    ppermute x4 -> x17, waiting for transfers between devices: 10.8 us -> 108 us  [the longest x9 67 us: to_mate(): return lax.ppermute(array, 'expert', mates)]
    pallas_call x0 -> x16, Pallas kernels: none -> 42.5 us  [the longest x4 21.2 us: hidden(): pl.pallas_call(hidden_kernel, grid=(width // block,), in_specs=[pl.BlockS...]
    dot_general x6 -> x0, matrix products: 33.8 us -> none  [the longest x2 26.2 us: expert_part(): jnp.dot(active, down_rows, preferred_element_type=jnp.float32)]
    all_to_all x2 -> x8, starting transfers between devices: 12.4 us -> 41.4 us  [across(): lax.all_to_all(array, 'expert', 0, 0, axis_index_groups=sides, tiled=True)]
    unnamed x4 -> x80, local copies, waits for them, and re-layouts: 5.43 us -> 31.5 us
    ppermute x4 -> x17, starting transfers between devices: 28.3 us -> 38.9 us  [the longest x8 30.4 us: to_section(): lax.ppermute(array, ('section', 'expert'), [(s * lanes + i, (s + by) % se...]
  transfers between devices with their start and end apart: 6 -> 25, of which waited for: 6 -> 20; matrix products, arithmetic and copies ran while one was open for 1% -> 3% of each run, Pallas kernels for 0% -> 13%
where the time goes in v1:
time: 311 us; the launch traced here: 309 us
  waiting for transfers between devices  139 us (45%)
  starting transfers between devices  80.3 us (26%)
  Pallas kernels  42.5 us (14%)
  local copies, waits for them, and re-layouts  41.4 us (13%)
  other arithmetic  4.44 us (1%)
    ppermute x9, waiting for transfers between devices, to_mate(): return lax.ppermute(array, 'expert', mates)  67 us
    all_to_all x8, starting transfers between devices, across(): lax.all_to_all(array, 'expert', 0, 0, axis_index_groups=sides, tiled=True)  41.4 us
    ppermute x8, waiting for transfers between devices, to_section(): lax.ppermute(array, ('section', 'expert'), [(s * lanes + i, (s + by) % se...  41.4 us
    unnamed x80, local copies, waits for them, and re-layouts  31.5 us
    all_to_all x8, waiting for transfers between devices, across(): lax.all_to_all(array, 'expert', 0, 0, axis_index_groups=sides, tiled=True)  30.6 us
    ppermute x8, starting transfers between devices, to_section(): lax.ppermute(array, ('section', 'expert'), [(s * lanes + i, (s + by) % se...  30.4 us
    pallas_call x4, Pallas kernels, hidden(): pl.pallas_call(hidden_kernel, grid=(width // block,), in_specs=[pl.BlockS...  21.2 us
    pallas_call x4, Pallas kernels, down(): pl.pallas_call(down_kernel, grid=(width // block,), in_specs=[whole, whol...  9.51 us
  transfers between devices with their start and end apart: 25, of which 20 were waited for; matrix products, arithmetic and copies ran while one was open for 3% of the time, Pallas kernels for 13%

profile of v1, /device:TPU:73, one launch (start us, length us, event | category | flops | bytes accessed | tf_op | source)
XLA Modules:
  0.0 308.8 jit_solution(15601069967782375353)
XLA Ops:
  7.1 8.9 %collective-permute-done.1.mate_ref = bf16[64,3584]{1,0:T(8,128)(2,1)S(1)} collective-permute-done((bf16[64,3584]{1,0:T(8,128)(2,1)}, bf16[64,3584]{1,0:T(8,128)(2,1)S(1)}, u32[]{:S(2)}, u32[]{:S(2)}) %collective-permute-start.1) | collective-permute-done | bytes 458784 | tf_op jit(solution)/shard_map/ppermute | solution.py:174
  17.2 2.5 shard_map.122
  19.7 5.5 %all-to-all-start = ((bf16[8,48,3584]{2,1,0:T(8,128)(2,1)}), bf16[8,48,3584]{2,1,0:T(8,128)(2,1)}, u32[]{:S(2)}, u32[]{:S(2)}) async-start(bf16[8,48,3584]{2,1,0:T(8,128)(2,1)} %bitcast.22), calls=%async_computation | async-start | bytes 5505024 | tf_op jit(solution)/shard_map/all_to_all | solution.py:217
  26.4 2.3 dynamic-slice_bitcast_fusion
  28.7 6.5 %collective-permute-done.2.mate_ref = bf16[64,3584]{1,0:T(8,128)(2,1)S(1)} collective-permute-done((bf16[64,3584]{1,0:T(8,128)(2,1)S(1)}, bf16[64,3584]{1,0:T(8,128)(2,1)S(1)}, u32[]{:S(2)}, u32[]{:S(2)}) %collective-permute-start.2) | collective-permute-done | bytes 458784 | tf_op jit(solution)/shard_map/ppermute | solution.py:174
  41.0 14.1 %collective-permute-done.3.refs_0_ = bf16[256,1792]{1,0:T(8,128)(2,1)S(1)} collective-permute-done((bf16[256,1792]{1,0:T(8,128)(2,1)S(1)}, bf16[256,1792]{1,0:T(8,128)(2,1)S(1)}, u32[]{:S(2)}, u32[]{:S(2)}) %collective-permute-start.3) | collective-permute-done | bytes 917536 | tf_op jit(solution)/shard_map/ppermute | solution.py:174
  55.1 3.4 %all-to-all-done = bf16[8,48,3584]{2,1,0:T(8,128)(2,1)} async-done(((bf16[8,48,3584]{2,1,0:T(8,128)(2,1)}), bf16[8,48,3584]{2,1,0:T(8,128)(2,1)}, u32[]{:S(2)}, u32[]{:S(2)}) %all-to-all-start) | async-done | bytes 2752544 | tf_op jit(solution)/shard_map/all_to_all | solution.py:217
  58.4 4.4 %all-to-all-start.1 = ((bf16[8,48,3584]{2,1,0:T(8,128)(2,1)}), bf16[8,48,3584]{2,1,0:T(8,128)(2,1)}, u32[]{:S(2)}, u32[]{:S(2)}) async-start(bf16[8,48,3584]{2,1,0:T(8,128)(2,1)} %bitcast.84), calls=%async_computation.1 | async-start | bytes 5505024 | tf_op jit(solution)/shard_map/all_to_all | solution.py:217
  65.8 2.0 copy-done
  67.8 2.0 copy-done.4
  69.8 5.3 %shard_map.124.own_ref = bf16[384,512]{1,0:T(8,128)(2,1)S(1)} custom-call(bf16[384,3584]{1,0:T(8,128)(2,1)} %bitcast.23.rows_ref, bf16[3584,512]{1,0:T(8,128)(2,1)S(1)} %bitcast.75, bf16[3584,512]{1,0:T(8,128)(2,1)S(1)} %bitcast.79), custom_call_target="tpu_custom_call" | custom-call | flops 2818572288 | bytes 10485760 | tf_op jit(solution)/shard_map/pallas_call | solution.py:76
  75.2 8.0 %collective-permute-done.5.refs_1_ = bf16[256,1792]{1,0:T(8,128)(2,1)S(1)} collective-permute-done((bf16[256,1792]{1,0:T(8,128)(2,1)S(1)}, bf16[256,1792]{1,0:T(8,128)(2,1)S(1)}, u32[]{:S(2)}, u32[]{:S(2)}) %collective-permute-start.5) | collective-permute-done | bytes 917536 | tf_op jit(solution)/shard_map/ppermute | solution.py:174
  83.3 8.4 %collective-permute-done.4.mate_ref = bf16[384,512]{1,0:T(8,128)(2,1)S(1)} collective-permute-done((bf16[384,512]{1,0:T(8,128)(2,1)S(1)}, bf16[384,512]{1,0:T(8,128)(2,1)S(1)}, u32[]{:S(2)}, u32[]{:S(2)}) %collective-permute-start.4) | collective-permute-done | bytes 393248 | tf_op jit(solution)/shard_map/ppermute | solution.py:174
  91.7 2.4 shard_map.125
  96.1 5.5 %all-to-all-start.2 = ((bf16[8,48,1792]{2,1,0:T(8,128)(2,1)}), bf16[8,48,1792]{2,1,0:T(8,128)(2,1)}, u32[]{:S(2)}, u32[]{:S(2)}) async-start(bf16[8,48,1792]{2,1,0:T(8,128)(2,1)} %bitcast.89), calls=%async_computation.2 | async-start | bytes 2752512 | tf_op jit(solution)/shard_map/all_to_all | solution.py:217
  101.6 2.0 copy-done.1
  103.6 2.0 copy-done.5
  105.6 5.3 %shard_map.126.own_ref = bf16[384,512]{1,0:T(8,128)(2,1)S(1)} custom-call(bf16[384,3584]{1,0:T(8,128)(2,1)} %bitcast.28.rows_ref, bf16[3584,512]{1,0:T(8,128)(2,1)S(1)} %bitcast.76, bf16[3584,512]{1,0:T(8,128)(2,1)S(1)} %bitcast.80), custom_call_target="tpu_custom_call" | custom-call | flops 2818572288 | bytes 10485760 | tf_op jit(solution)/shard_map/pallas_call | solution.py:76
  110.9 1.9 collective-permute-start.6
  115.1 3.3 %collective-permute-done.6.mate_ref = bf16[384,512]{1,0:T(8,128)(2,1)S(1)} collective-permute-done((bf16[384,512]{1,0:T(8,128)(2,1)S(1)}, bf16[384,512]{1,0:T(8,128)(2,1)S(1)}, u32[]{:S(2)}, u32[]{:S(2)}) %collective-permute-start.6) | collective-permute-done | bytes 393248 | tf_op jit(solution)/shard_map/ppermute | solution.py:174
  119.5 2.4 shard_map.127
  123.1 5.9 %all-to-all-start.3 = ((bf16[8,48,1792]{2,1,0:T(8,128)(2,1)}), bf16[8,48,1792]{2,1,0:T(8,128)(2,1)}, u32[]{:S(2)}, u32[]{:S(2)}) async-start(bf16[8,48,1792]{2,1,0:T(8,128)(2,1)} %bitcast.88), calls=%async_computation.3 | async-start | bytes 2752512 | tf_op jit(solution)/shard_map/all_to_all | solution.py:217
  132.1 9.3 %collective-permute-start.8 = (bf16[128,1792]{1,0:T(8,128)(2,1)S(1)}, bf16[128,1792]{1,0:T(8,128)(2,1)S(1)}, u32[]{:S(2)}, u32[]{:S(2)}) collective-permute-start(bf16[128,1792]{1,0:T(8,128)(2,1)S(1)} %shard_map.128), channel_id=1, source_target_pairs={{0,17},{1,16},{2,19},{3,18},{4,21},{5,20},{6,23},{7,22},{8,25},{9,... | collective-permute-start | bytes 1376264 | tf_op jit(solution)/shard_map/ppermute | solution.py:178
  141.4 9.7 %collective-permute-done.8.far_ref = bf16[128,1792]{1,0:T(8,128)(2,1)S(1)} collective-permute-done((bf16[128,1792]{1,0:T(8,128)(2,1)S(1)}, bf16[128,1792]{1,0:T(8,128)(2,1)S(1)}, u32[]{:S(2)}, u32[]{:S(2)}) %collective-permute-start.8) | collective-permute-done | bytes 458784 | tf_op jit(solution)/shard_map/ppermute | solution.py:178
  155.3 6.2 %all-to-all-start.4 = ((bf16[8,48,3584]{2,1,0:T(8,128)(2,1)}), bf16[8,48,3584]{2,1,0:T(8,128)(2,1)}, u32[]{:S(2)}, u32[]{:S(2)}) async-start(bf16[8,48,3584]{2,1,0:T(8,128)(2,1)} %bitcast.83), calls=%async_computation.4 | async-start | bytes 5505024 | tf_op jit(solution)/shard_map/all_to_all | solution.py:217
  165.9 9.3 %collective-permute-done.10.far_ref = bf16[128,1792]{1,0:T(8,128)(2,1)S(1)} collective-permute-done((bf16[128,1792]{1,0:T(8,128)(2,1)S(1)}, bf16[128,1792]{1,0:T(8,128)(2,1)S(1)}, u32[]{:S(2)}, u32[]{:S(2)}) %collective-permute-start.10) | collective-permute-done | bytes 458784 | tf_op jit(solution)/shard_map/ppermute | solution.py:178
  175.2 3.7 %collective-permute-done.9.near_ref.state_ref = bf16[128,1792]{1,0:T(8,128)(2,1)S(1)} collective-permute-done((bf16[128,1792]{1,0:T(8,128)(2,1)S(1)}, bf16[128,1792]{1,0:T(8,128)(2,1)S(1)}, u32[]{:S(2)}, u32[]{:S(2)}) %collective-permute-start.9) | collective-permute-done | bytes 458784 | tf_op jit(solution)/shard_map/ppermute | solution.py:178
  181.7 15.3 %all-to-all-done.4 = bf16[8,48,3584]{2,1,0:T(8,128)(2,1)} async-done(((bf16[8,48,3584]{2,1,0:T(8,128)(2,1)}), bf16[8,48,3584]{2,1,0:T(8,128)(2,1)}, u32[]{:S(2)}, u32[]{:S(2)}) %all-to-all-start.4) | async-done | bytes 2752544 | tf_op jit(solution)/shard_map/all_to_all | solution.py:217
  197.0 5.4 %all-to-all-start.5 = ((bf16[8,48,3584]{2,1,0:T(8,128)(2,1)}), bf16[8,48,3584]{2,1,0:T(8,128)(2,1)}, u32[]{:S(2)}, u32[]{:S(2)}) async-start(bf16[8,48,3584]{2,1,0:T(8,128)(2,1)} %bitcast.85), calls=%async_computation.5 | async-start | bytes 5505024 | tf_op jit(solution)/shard_map/all_to_all | solution.py:217
  202.4 2.0 copy-done.2
  204.5 2.0 copy-done.6
  206.5 5.3 %shard_map.132.own_ref = bf16[384,512]{1,0:T(8,128)(2,1)S(1)} custom-call(bf16[384,3584]{1,0:T(8,128)(2,1)} %bitcast.38.rows_ref, bf16[3584,512]{1,0:T(8,128)(2,1)S(1)} %bitcast.77, bf16[3584,512]{1,0:T(8,128)(2,1)S(1)} %bitcast.81), custom_call_target="tpu_custom_call" | custom-call | flops 2818572288 | bytes 10485760 | tf_op jit(solution)/shard_map/pallas_call | solution.py:76
  212.2 8.0 %collective-permute-done.11.mate_ref = bf16[384,512]{1,0:T(8,128)(2,1)S(1)} collective-permute-done((bf16[384,512]{1,0:T(8,128)(2,1)S(1)}, bf16[384,512]{1,0:T(8,128)(2,1)S(1)}, u32[]{:S(2)}, u32[]{:S(2)}) %collective-permute-start.11) | collective-permute-done | bytes 393248 | tf_op jit(solution)/shard_map/ppermute | solution.py:174
  220.2 2.4 shard_map.133
  223.7 12.0 %all-to-all-done.5 = bf16[8,48,3584]{2,1,0:T(8,128)(2,1)} async-done(((bf16[8,48,3584]{2,1,0:T(8,128)(2,1)}), bf16[8,48,3584]{2,1,0:T(8,128)(2,1)}, u32[]{:S(2)}, u32[]{:S(2)}) %all-to-all-start.5) | async-done | bytes 2752544 | tf_op jit(solution)/shard_map/all_to_all | solution.py:217
  235.7 4.3 %all-to-all-start.6 = ((bf16[8,48,1792]{2,1,0:T(8,128)(2,1)}), bf16[8,48,1792]{2,1,0:T(8,128)(2,1)}, u32[]{:S(2)}, u32[]{:S(2)}) async-start(bf16[8,48,1792]{2,1,0:T(8,128)(2,1)} %bitcast.90), calls=%async_computation.6 | async-start | bytes 2752512 | tf_op jit(solution)/shard_map/all_to_all | solution.py:217
  240.0 2.0 copy-done.3
  242.0 2.0 copy-done.7
  244.1 5.3 %shard_map.134.own_ref = bf16[384,512]{1,0:T(8,128)(2,1)S(1)} custom-call(bf16[384,3584]{1,0:T(8,128)(2,1)} %bitcast.40.rows_ref, bf16[3584,512]{1,0:T(8,128)(2,1)S(1)} %bitcast.78, bf16[3584,512]{1,0:T(8,128)(2,1)S(1)} %bitcast.82), custom_call_target="tpu_custom_call" | custom-call | flops 2818572288 | bytes 10485760 | tf_op jit(solution)/shard_map/pallas_call | solution.py:76
  249.8 9.0 %collective-permute-done.12.mate_ref = bf16[384,512]{1,0:T(8,128)(2,1)S(1)} collective-permute-done((bf16[384,512]{1,0:T(8,128)(2,1)S(1)}, bf16[384,512]{1,0:T(8,128)(2,1)S(1)}, u32[]{:S(2)}, u32[]{:S(2)}) %collective-permute-start.12) | collective-permute-done | bytes 393248 | tf_op jit(solution)/shard_map/ppermute | solution.py:174
  258.8 2.4 shard_map.135
  262.3 4.3 %all-to-all-start.7 = ((bf16[8,48,1792]{2,1,0:T(8,128)(2,1)}), bf16[8,48,1792]{2,1,0:T(8,128)(2,1)S(1)}, u32[]{:S(2)}, u32[]{:S(2)}) async-start(bf16[8,48,1792]{2,1,0:T(8,128)(2,1)} %bitcast.86), calls=%async_computation.7 | async-start | bytes 2752512 | tf_op jit(solution)/shard_map/all_to_all | solution.py:217
  266.8 1.8 shard_map.136
  268.7 17.3 %collective-permute-start.13 = (bf16[64,1792]{1,0:T(8,128)(2,1)S(1)}, bf16[64,1792]{1,0:T(8,128)(2,1)S(1)}, u32[]{:S(2)}, u32[]{:S(2)}) collective-permute-start(bf16[64,1792]{1,0:T(8,128)(2,1)S(1)} %get-tuple-element.56), channel_id=1, source_target_pairs={{0,16},{1,17},{2,18},{3,19},{4,20},{5,21},{6,22},{7,23},{8,24},{9,... | collective-permute-start | bytes 688136 | tf_op jit(solution)/shard_map/ppermute | solution.py:178
  286.0 1.9 collective-permute-start.14
  289.0 2.5 collective-permute-done.14
  293.4 10.6 %collective-permute-done.15 = bf16[64,1792]{1,0:T(8,128)(2,1)S(1)} collective-permute-done((bf16[64,1792]{1,0:T(8,128)(2,1)S(1)}, bf16[64,1792]{1,0:T(8,128)(2,1)S(1)}, u32[]{:S(2)}, u32[]{:S(2)}) %collective-permute-start.15) | collective-permute-done | bytes 229408 | tf_op jit(solution)/shard_map/ppermute | solution.py:178
  304.0 4.0 %collective-permute-done.16 = bf16[64,1792]{1,0:T(8,128)(2,1)S(1)} collective-permute-done((bf16[64,1792]{1,0:T(8,128)(2,1)S(1)}, bf16[64,1792]{1,0:T(8,128)(2,1)S(1)}, u32[]{:S(2)}, u32[]{:S(2)}) %collective-permute-start.16) | collective-permute-done | bytes 229408 | tf_op jit(solution)/shard_map/ppermute | solution.py:178
  (146 shorter events, 45.7 us)
Async XLA Ops:
  3.8 2.5 collective-permute-start
  4.4 11.6 %collective-permute-start.1 = (bf16[64,3584]{1,0:T(8,128)(2,1)}, bf16[64,3584]{1,0:T(8,128)(2,1)S(1)}, u32[]{:S(2)}, u32[]{:S(2)}) collective-permute-start(bf16[64,3584]{1,0:T(8,128)(2,1)} %bitcast.91), channel_id=1, source_target_pairs={{0,1},{1,0},{2,3},{3,2},{4,5},{5,4},{6,7},{7,6},{8,9},{9,8},{10,11... | collective-permute-start | bytes 1376264 | tf_op jit(solution)/shard_map/ppermute | solution.py:174
  6.4 13.3 %copy-start.35 = (f32[8,64]{1,0:T(8,128)}, f32[8,64]{1,0:T(8,128)S(1)}, u32[]{:S(2)}) copy-start(f32[8,64]{1,0:T(8,128)S(1)} %collective-permute-done) | copy-start | bytes 6148
  16.0 3.7 %copy-start.24 = (bf16[64,3584]{1,0:T(8,128)(2,1)}, bf16[64,3584]{1,0:T(8,128)(2,1)S(1)}, u32[]{:S(2)}) copy-start(bf16[64,3584]{1,0:T(8,128)(2,1)S(1)} %collective-permute-done.1.mate_ref) | copy-start | bytes 1376260
  19.7 5.5 %copy-start.22 = (bf16[1,64,3584]{2,1,0:T(8,128)(2,1)S(1)}, bf16[1,64,3584]{2,1,0:T(8,128)(2,1)}, u32[]{:S(2)}) copy-start(bf16[1,64,3584]{2,1,0:T(8,128)(2,1)} %param.12) | copy-start | bytes 1376260
  19.7 38.7 %all-to-all-start = ((bf16[8,48,3584]{2,1,0:T(8,128)(2,1)}), bf16[8,48,3584]{2,1,0:T(8,128)(2,1)}, u32[]{:S(2)}, u32[]{:S(2)}) async-start(bf16[8,48,3584]{2,1,0:T(8,128)(2,1)} %bitcast.22), calls=%async_computation | async-start | bytes 5505024 | tf_op jit(solution)/shard_map/all_to_all | solution.py:217
  25.2 10.0 %collective-permute-start.2 = (bf16[64,3584]{1,0:T(8,128)(2,1)S(1)}, bf16[64,3584]{1,0:T(8,128)(2,1)S(1)}, u32[]{:S(2)}, u32[]{:S(2)}) collective-permute-start(bf16[64,3584]{1,0:T(8,128)(2,1)S(1)} %bitcast.93), channel_id=1, source_target_pairs={{0,1},{1,0},{2,3},{3,2},{4,5},{5,4},{6,7},{7,6},{8,9},{9,8},{10,11... | collective-permute-start | bytes 1376264 | tf_op jit(solution)/shard_map/ppermute | solution.py:174
  28.7 8.6 %copy-start.28 = (bf16[512,1792]{1,0:T(8,128)(2,1)}, bf16[512,1792]{1,0:T(8,128)(2,1)S(1)}, u32[]{:S(2)}) copy-start(bf16[512,1792]{1,0:T(8,128)(2,1)S(1)} %get-tuple-element.30) | copy-start | bytes 5505028
  36.0 19.0 %collective-permute-start.3 = (bf16[256,1792]{1,0:T(8,128)(2,1)S(1)}, bf16[256,1792]{1,0:T(8,128)(2,1)S(1)}, u32[]{:S(2)}, u32[]{:S(2)}) collective-permute-start(bf16[256,1792]{1,0:T(8,128)(2,1)S(1)} %slice.83), channel_id=1, source_target_pairs={{0,1},{1,0},{2,3},{3,2},{4,5},{5,4},{6,7},{7,6},{8,9},{9,8},{10,11... | collective-permute-start | bytes 2752520 | tf_op jit(solution)/shard_map/ppermute | solution.py:174
  58.4 37.6 %all-to-all-start.1 = ((bf16[8,48,3584]{2,1,0:T(8,128)(2,1)}), bf16[8,48,3584]{2,1,0:T(8,128)(2,1)}, u32[]{:S(2)}, u32[]{:S(2)}) async-start(bf16[8,48,3584]{2,1,0:T(8,128)(2,1)} %bitcast.84), calls=%async_computation.1 | async-start | bytes 5505024 | tf_op jit(solution)/shard_map/all_to_all | solution.py:217
  64.1 19.2 %collective-permute-start.5 = (bf16[256,1792]{1,0:T(8,128)(2,1)S(1)}, bf16[256,1792]{1,0:T(8,128)(2,1)S(1)}, u32[]{:S(2)}, u32[]{:S(2)}) collective-permute-start(bf16[256,1792]{1,0:T(8,128)(2,1)S(1)} %slice.84), channel_id=1, source_target_pairs={{0,1},{1,0},{2,3},{3,2},{4,5},{5,4},{6,7},{7,6},{8,9},{9,8},{10,11... | collective-permute-start | bytes 2752520 | tf_op jit(solution)/shard_map/ppermute | solution.py:174
  65.8 2.0 copy-start
  67.8 2.0 copy-start.4
  75.1 16.6 %collective-permute-start.4 = (bf16[384,512]{1,0:T(8,128)(2,1)S(1)}, bf16[384,512]{1,0:T(8,128)(2,1)S(1)}, u32[]{:S(2)}, u32[]{:S(2)}) collective-permute-start(bf16[384,512]{1,0:T(8,128)(2,1)S(1)} %shard_map.124.own_ref), channel_id=1, source_target_pairs={{0,1},{1,0},{2,3},{3,2},{4,5},{5,4},{6,7},{7,6},{8,9},{9,8},{10,11... | collective-permute-start | bytes 1179656 | tf_op jit(solution)/shard_map/ppermute | solution.py:174
  96.1 27.0 %all-to-all-start.2 = ((bf16[8,48,1792]{2,1,0:T(8,128)(2,1)}), bf16[8,48,1792]{2,1,0:T(8,128)(2,1)}, u32[]{:S(2)}, u32[]{:S(2)}) async-start(bf16[8,48,1792]{2,1,0:T(8,128)(2,1)} %bitcast.89), calls=%async_computation.2 | async-start | bytes 2752512 | tf_op jit(solution)/shard_map/all_to_all | solution.py:217
  101.6 2.0 copy-start.1
  103.6 2.0 copy-start.5
  110.9 7.4 %collective-permute-start.6 = (bf16[384,512]{1,0:T(8,128)(2,1)S(1)}, bf16[384,512]{1,0:T(8,128)(2,1)S(1)}, u32[]{:S(2)}, u32[]{:S(2)}) collective-permute-start(bf16[384,512]{1,0:T(8,128)(2,1)S(1)} %shard_map.126.own_ref), channel_id=1, source_target_pairs={{0,1},{1,0},{2,3},{3,2},{4,5},{5,4},{6,7},{7,6},{8,9},{9,8},{10,11... | collective-permute-start | bytes 1179656 | tf_op jit(solution)/shard_map/ppermute | solution.py:174
  123.0 5.9 %copy-start.30 = (f32[1,64]{1,0:T(1,128)S(1)}, f32[1,64]{1,0:T(1,128)}, u32[]{:S(2)}) copy-start(f32[1,64]{1,0:T(1,128)} %copy-done.29) | copy-start | bytes 772
  123.0 5.9 %copy-start.32 = (f32[1,64]{1,0:T(1,128)S(1)}, f32[1,64]{1,0:T(1,128)}, u32[]{:S(2)}) copy-start(f32[1,64]{1,0:T(1,128)} %copy-done.31) | copy-start | bytes 772
  123.0 5.9 %copy-start.34 = (f32[1,64]{1,0:T(1,128)S(1)}, f32[1,64]{1,0:T(1,128)}, u32[]{:S(2)}) copy-start(f32[1,64]{1,0:T(1,128)} %copy-done.33) | copy-start | bytes 772
  123.0 6.0 %copy-start.39 = (s32[128,1]{0,1:T(1,128)S(1)}, s32[128,1]{0,1:T(1,128)}, u32[]{:S(2)}) copy-start(s32[128,1]{0,1:T(1,128)} %get-tuple-element.76) | copy-start | bytes 1540
  123.0 6.3 %copy-start.25 = (bf16[64,3584]{1,0:T(8,128)(2,1)S(1)}, bf16[64,3584]{1,0:T(8,128)(2,1)}, u32[]{:S(2)}) copy-start(bf16[64,3584]{1,0:T(8,128)(2,1)} %copy-done.24) | copy-start | bytes 1376260
  123.1 32.3 %all-to-all-start.3 = ((bf16[8,48,1792]{2,1,0:T(8,128)(2,1)}), bf16[8,48,1792]{2,1,0:T(8,128)(2,1)}, u32[]{:S(2)}, u32[]{:S(2)}) async-start(bf16[8,48,1792]{2,1,0:T(8,128)(2,1)} %bitcast.88), calls=%async_computation.3 | async-start | bytes 2752512 | tf_op jit(solution)/shard_map/all_to_all | solution.py:217
  132.1 19.1 %collective-permute-start.8 = (bf16[128,1792]{1,0:T(8,128)(2,1)S(1)}, bf16[128,1792]{1,0:T(8,128)(2,1)S(1)}, u32[]{:S(2)}, u32[]{:S(2)}) collective-permute-start(bf16[128,1792]{1,0:T(8,128)(2,1)S(1)} %shard_map.128), channel_id=1, source_target_pairs={{0,17},{1,16},{2,19},{3,18},{4,21},{5,20},{6,23},{7,22},{8,25},{9,... | collective-permute-start | bytes 1376264 | tf_op jit(solution)/shard_map/ppermute | solution.py:178
  141.4 10.4 %collective-permute-start.7 = (bf16[128,1792]{1,0:T(8,128)(2,1)S(1)}, bf16[128,1792]{1,0:T(8,128)(2,1)S(1)}, u32[]{:S(2)}, u32[]{:S(2)}) collective-permute-start(bf16[128,1792]{1,0:T(8,128)(2,1)S(1)} %shard_map.128), channel_id=1, source_target_pairs={{0,16},{1,17},{2,18},{3,19},{4,20},{5,21},{6,22},{7,23},{8,24},{9,... | collective-permute-start | bytes 1376264 | tf_op jit(solution)/shard_map/ppermute | solution.py:178
  155.3 6.2 %copy-start.38 = (s32[128,1]{0,1:T(1,128)S(1)}, s32[128,1]{0,1:T(1,128)}, u32[]{:S(2)}) copy-start(s32[128,1]{0,1:T(1,128)} %get-tuple-element.77) | copy-start | bytes 1540
  155.3 6.4 %copy-start.23 = (bf16[1,64,3584]{2,1,0:T(8,128)(2,1)S(1)}, bf16[1,64,3584]{2,1,0:T(8,128)(2,1)}, u32[]{:S(2)}) copy-start(bf16[1,64,3584]{2,1,0:T(8,128)(2,1)} %param.12) | copy-start | bytes 1376260
  155.3 41.7 %all-to-all-start.4 = ((bf16[8,48,3584]{2,1,0:T(8,128)(2,1)}), bf16[8,48,3584]{2,1,0:T(8,128)(2,1)}, u32[]{:S(2)}, u32[]{:S(2)}) async-start(bf16[8,48,3584]{2,1,0:T(8,128)(2,1)} %bitcast.83), calls=%async_computation.4 | async-start | bytes 5505024 | tf_op jit(solution)/shard_map/all_to_all | solution.py:217
  164.6 10.7 %collective-permute-start.10 = (bf16[128,1792]{1,0:T(8,128)(2,1)S(1)}, bf16[128,1792]{1,0:T(8,128)(2,1)S(1)}, u32[]{:S(2)}, u32[]{:S(2)}) collective-permute-start(bf16[128,1792]{1,0:T(8,128)(2,1)S(1)} %shard_map.130), channel_id=1, source_target_pairs={{0,241},{1,240},{2,243},{3,242},{4,245},{5,244},{6,247},{7,246},{8... | collective-permute-start | bytes 1376264 | tf_op jit(solution)/shard_map/ppermute | solution.py:178
  164.9 14.0 %collective-permute-start.9 = (bf16[128,1792]{1,0:T(8,128)(2,1)S(1)}, bf16[128,1792]{1,0:T(8,128)(2,1)S(1)}, u32[]{:S(2)}, u32[]{:S(2)}) collective-permute-start(bf16[128,1792]{1,0:T(8,128)(2,1)S(1)} %shard_map.130), channel_id=1, source_target_pairs={{0,240},{1,241},{2,242},{3,243},{4,244},{5,245},{6,246},{7,247},{8... | collective-permute-start | bytes 1376264 | tf_op jit(solution)/shard_map/ppermute | solution.py:178
  197.0 38.7 %all-to-all-start.5 = ((bf16[8,48,3584]{2,1,0:T(8,128)(2,1)}), bf16[8,48,3584]{2,1,0:T(8,128)(2,1)}, u32[]{:S(2)}, u32[]{:S(2)}) async-start(bf16[8,48,3584]{2,1,0:T(8,128)(2,1)} %bitcast.85), calls=%async_computation.5 | async-start | bytes 5505024 | tf_op jit(solution)/shard_map/all_to_all | solution.py:217
  202.4 2.0 copy-start.2
  204.5 2.0 copy-start.6
  206.5 13.7 %copy-start.10 = (bf16[256,1792]{1,0:T(8,128)(2,1)S(1)}, bf16[256,1792]{1,0:T(8,128)(2,1)}, u32[]{:S(2)}) copy-start(bf16[256,1792]{1,0:T(8,128)(2,1)} %copy-done.8) | copy-start | bytes 2752516
  211.8 8.4 %collective-permute-start.11 = (bf16[384,512]{1,0:T(8,128)(2,1)S(1)}, bf16[384,512]{1,0:T(8,128)(2,1)S(1)}, u32[]{:S(2)}, u32[]{:S(2)}) collective-permute-start(bf16[384,512]{1,0:T(8,128)(2,1)S(1)} %shard_map.132.own_ref), channel_id=1, source_target_pairs={{0,1},{1,0},{2,3},{3,2},{4,5},{5,4},{6,7},{7,6},{8,9},{9,8},{10,11... | collective-permute-start | bytes 1179656 | tf_op jit(solution)/shard_map/ppermute | solution.py:174
  235.7 26.6 %all-to-all-start.6 = ((bf16[8,48,1792]{2,1,0:T(8,128)(2,1)}), bf16[8,48,1792]{2,1,0:T(8,128)(2,1)}, u32[]{:S(2)}, u32[]{:S(2)}) async-start(bf16[8,48,1792]{2,1,0:T(8,128)(2,1)} %bitcast.90), calls=%async_computation.6 | async-start | bytes 2752512 | tf_op jit(solution)/shard_map/all_to_all | solution.py:217
  240.0 2.0 copy-start.3
  244.1 14.7 %copy-start.11 = (bf16[256,1792]{1,0:T(8,128)(2,1)S(1)}, bf16[256,1792]{1,0:T(8,128)(2,1)}, u32[]{:S(2)}) copy-start(bf16[256,1792]{1,0:T(8,128)(2,1)} %copy-done.8) | copy-start | bytes 2752516
  249.4 9.4 %collective-permute-start.12 = (bf16[384,512]{1,0:T(8,128)(2,1)S(1)}, bf16[384,512]{1,0:T(8,128)(2,1)S(1)}, u32[]{:S(2)}, u32[]{:S(2)}) collective-permute-start(bf16[384,512]{1,0:T(8,128)(2,1)S(1)} %shard_map.134.own_ref), channel_id=1, source_target_pairs={{0,1},{1,0},{2,3},{3,2},{4,5},{5,4},{6,7},{7,6},{8,9},{9,8},{10,11... | collective-permute-start | bytes 1179656 | tf_op jit(solution)/shard_map/ppermute | solution.py:174
  262.3 4.3 %copy-start.37 = (s32[128,1]{0,1:T(1,128)S(1)}, s32[128,1]{0,1:T(1,128)}, u32[]{:S(2)}) copy-start(s32[128,1]{0,1:T(1,128)} %get-tuple-element.75) | copy-start | bytes 1540
  262.3 4.5 %copy-start.20 = (bf16[128,1792]{1,0:T(8,128)(2,1)S(1)}, bf16[128,1792]{1,0:T(8,128)(2,1)}, u32[]{:S(2)}) copy-start(bf16[128,1792]{1,0:T(8,128)(2,1)} %copy-done.19) | copy-start | bytes 1376260
  262.3 25.6 %copy-start.36 = (s32[128,1]{0,1:T(1,128)S(1)}, s32[128,1]{0,1:T(1,128)}, u32[]{:S(2)}) copy-start(s32[128,1]{0,1:T(1,128)} %get-tuple-element.74) | copy-start | bytes 1540
  262.3 29.2 %all-to-all-start.7 = ((bf16[8,48,1792]{2,1,0:T(8,128)(2,1)}), bf16[8,48,1792]{2,1,0:T(8,128)(2,1)S(1)}, u32[]{:S(2)}, u32[]{:S(2)}) async-start(bf16[8,48,1792]{2,1,0:T(8,128)(2,1)} %bitcast.86), calls=%async_computation.7 | async-start | bytes 2752512 | tf_op jit(solution)/shard_map/all_to_all | solution.py:217
  268.7 20.3 %collective-permute-start.13 = (bf16[64,1792]{1,0:T(8,128)(2,1)S(1)}, bf16[64,1792]{1,0:T(8,128)(2,1)S(1)}, u32[]{:S(2)}, u32[]{:S(2)}) collective-permute-start(bf16[64,1792]{1,0:T(8,128)(2,1)S(1)} %get-tuple-element.56), channel_id=1, source_target_pairs={{0,16},{1,17},{2,18},{3,19},{4,20},{5,21},{6,22},{7,23},{8,24},{9,... | collective-permute-start | bytes 688136 | tf_op jit(solution)/shard_map/ppermute | solution.py:178
  286.0 5.4 %collective-permute-start.14 = (bf16[64,1792]{1,0:T(8,128)(2,1)S(1)}, bf16[64,1792]{1,0:T(8,128)(2,1)S(1)}, u32[]{:S(2)}, u32[]{:S(2)}) collective-permute-start(bf16[64,1792]{1,0:T(8,128)(2,1)S(1)} %get-tuple-element.57), channel_id=1, source_target_pairs={{0,17},{1,16},{2,19},{3,18},{4,21},{5,20},{6,23},{7,22},{8,25},{9,... | collective-permute-start | bytes 688136 | tf_op jit(solution)/shard_map/ppermute | solution.py:178
  292.0 12.0 %collective-permute-start.15 = (bf16[64,1792]{1,0:T(8,128)(2,1)S(1)}, bf16[64,1792]{1,0:T(8,128)(2,1)S(1)}, u32[]{:S(2)}, u32[]{:S(2)}) collective-permute-start(bf16[64,1792]{1,0:T(8,128)(2,1)S(1)} %get-tuple-element.52), channel_id=1, source_target_pairs={{0,240},{1,241},{2,242},{3,243},{4,244},{5,245},{6,246},{7,247},{8... | collective-permute-start | bytes 688136 | tf_op jit(solution)/shard_map/ppermute | solution.py:178
  292.6 15.4 %collective-permute-start.16 = (bf16[64,1792]{1,0:T(8,128)(2,1)S(1)}, bf16[64,1792]{1,0:T(8,128)(2,1)S(1)}, u32[]{:S(2)}, u32[]{:S(2)}) collective-permute-start(bf16[64,1792]{1,0:T(8,128)(2,1)S(1)} %get-tuple-element.53), channel_id=1, source_target_pairs={{0,241},{1,240},{2,243},{3,242},{4,245},{5,244},{6,247},{7,246},{8... | collective-permute-start | bytes 688136 | tf_op jit(solution)/shard_map/ppermute | solution.py:178
  (17 other events, 18.7 us)

commit v2 on v1

--- a/solution.py
+++ b/solution.py
@@ -31,8 +31,10 @@
     return packed
 
 
-def first_pack_kernel(slots_ref, own_ref, mate_ref, out_ref):
-    rows = jnp.concatenate([own_ref[...], mate_ref[...]], axis=0)
+def first_pack_kernel(slots_ref, own_ref, *refs):
+    mate_refs, out_ref = refs[:-1], refs[-1]
+    mate = sum(ref[...].astype(jnp.float32) for ref in mate_refs).astype(jnp.bfloat16)
+    rows = jnp.concatenate([own_ref[...], mate], axis=0)
     out_ref[...] = normed_select(slots_ref[...], [rows], out_ref.shape[0])[0]
 
 
@@ -83,7 +85,7 @@
         ],
         out_specs=pl.BlockSpec((count, block), lambda j: (0, j)),
         out_shape=jax.ShapeDtypeStruct((count, width), jnp.bfloat16),
-        compiler_params=pltpu.CompilerParams(vmem_limit_bytes=32 * MIB),
+        compiler_params=pltpu.CompilerParams(vmem_limit_bytes=56 * MIB),
         cost_estimate=pl.CostEstimate(
             flops=4 * count * features * width,
             bytes_accessed=2 * (count * features + 2 * features * width + count * width),
@@ -148,7 +150,7 @@
             bytes_accessed=2 * (2 * rows + count) * half,
             transcendentals=0,
         ),
-    )(live, slots.reshape(rows, 1), scale.reshape(rows, 1), state, returned)
+    )(live, slots, scale, state, returned)
 
 
 def local(forward_in, reverse_in, w_gate, w_up, w_down, routes, gate_weight):
@@ -164,7 +166,7 @@
     lane = lax.axis_index("expert")
     side = lane % 2
     group = jnp.where((lane % 4 == 0) | (lane % 4 == 3), 0, 1)
-    order = [0, 4, 3, 7, 1, 5, 2, 6]
+    order = [0, 2, 4, 6, 5, 7, 1, 3]
     members = [2 * e if e % 2 == 0 else 2 * e + 1 for e in order]
     sides = [members, [i ^ 1 for i in members]]
     place = [order.index(e) for e in range(experts)]
@@ -172,6 +174,13 @@
 
     def to_mate(array):
         return lax.ppermute(array, "expert", mates)
+
+    def to_mate_of(array, parity):
+        return lax.ppermute(
+            array,
+            ("section", "expert"),
+            [(s * lanes + i, s * lanes + (i ^ 1)) for s in range(parity, sections, 2) for i in range(lanes)],
+        )
 
     def to_section(array, direction, cross):
         by = -1 if direction else 1
@@ -198,10 +207,14 @@
     plans = [plan(direction, tick) for direction in range(2) for tick in range(tick_count)]
     own_plan = jnp.stack([p[0].astype(jnp.float32) for p in plans] + [p[1] for p in plans])
     mate_plan = to_mate(own_plan)
+    late_forward, mate_plan = together(forward_in[0], mate_plan)
     own_slots = own_plan[: len(plans)].astype(jnp.int32) + side * most_rows
     mate_slots = mate_plan[: len(plans)].astype(jnp.int32) + (1 - side) * most_rows
     slots = jnp.concatenate([own_slots, mate_slots], axis=1)
     scales = jnp.concatenate([own_plan[len(plans) :], mate_plan[len(plans) :]], axis=1)
+    columns = [
+        (slots[at].reshape(-1, 1), scales[at].reshape(-1, 1)) for at in range(len(plans))
+    ]
     group_flag = group.astype(jnp.int32).reshape(1, 1)
 
     def pair_slots(direction, tick):
@@ -210,7 +223,7 @@
     gate_cols, up_cols, down_rows = w_gate[0], w_up[0], w_down[0]
     down_own = lax.dynamic_slice_in_dim(down_rows, group * half, half, 1)
     down_other = lax.dynamic_slice_in_dim(down_rows, (1 - group) * half, half, 1)
-    depth = down_rows.shape[0] // 2
+    depth = down_rows.shape[0] * 19 // 32
 
     def across(array):
         array = array.reshape(experts, 2 * most_rows, array.shape[-1])
@@ -229,7 +242,7 @@
 
     def finish(direction, tick, near, returned):
         at = direction * tick_count + tick
-        return merge(plans[at][2], slots[at], scales[at], near, returned)
+        return merge(plans[at][2], *columns[at], near, returned)
 
     def repack(direction, tick, near, far):
         operands = (group_flag, pair_slots(direction, tick), near, far)
@@ -243,13 +256,14 @@
             [jnp.where(first, own, mate), jnp.where(first, mate, own)], axis=1
         )[None]
 
-    def first_pack(direction, own, mate):
-        operands = (pair_slots(direction, 0), own, mate)
+    def first_pack(direction, own, *mate):
+        operands = (pair_slots(direction, 0), own, *mate)
         return pack(first_pack_kernel, slot_total, features, *operands)
 
     forward, reverse = forward_in[0], reverse_in[0]
-    forward_mate = to_mate(forward)
-    packed_forward = first_pack(0, forward, forward_mate)
+    forward_mates = [to_mate_of(forward, 1), to_mate_of(late_forward, 0)]
+    packed_forward = first_pack(0, forward, *forward_mates)
+    forward_mate = forward_mates[0] + forward_mates[1]
     reverse, packed_forward = together(reverse, packed_forward)
     reverse_mate = to_mate(reverse)
     reverse_mate, down_other = together(reverse_mate, down_other)
@@ -264,8 +278,8 @@
             packed_reverse = first_pack(1, reverse, reverse_mate)
             reverse_near = near_half(reverse, reverse_mate)
             forward_near = near_half(forward, forward_mate)
-            packed_reverse, down_mate[0], down_other = together(
-                packed_reverse, down_mate[0], down_other
+            packed_reverse, down_mate[0], down_other, forward_near, reverse_near, columns = together(
+                packed_reverse, down_mate[0], down_other, forward_near, reverse_near, columns
             )
             down_mate.append(to_mate(down_other[depth:]))
         packed_reverse, received = together(packed_reverse, received)

time: 311 us -> 295 us (0.949)
  local copies, waits for them, and re-layouts: 41.4 us -> 23.2 us
  waiting for transfers between devices: 139 us -> 129 us
  Pallas kernels: 42.5 us -> 50.3 us
  starting transfers between devices: 80.3 us -> 85.5 us
    unnamed x80 -> x48, local copies, waits for them, and re-layouts: 31.5 us -> 17.1 us
    ppermute x9 -> x8, waiting for transfers between devices: 67 us -> 57.7 us  [to_mate(): return lax.ppermute(array, 'expert', mates)]
    ppermute x0 -> x2, waiting for transfers between devices: none -> 6.28 us  [to_mate_of(): lax.ppermute(array, ('section', 'expert'), [(s * lanes + i, s * lanes + (...]
    pallas_call x4, Pallas kernels: 21.2 us -> 27.4 us  [hidden(): pl.pallas_call(hidden_kernel, grid=(width // block,), in_specs=[pl.BlockS...]
    all_to_all x8, waiting for transfers between devices: 30.6 us -> 26.2 us  [across(): lax.all_to_all(array, 'expert', 0, 0, axis_index_groups=sides, tiled=True)]
    ppermute x0 -> x2, starting transfers between devices: none -> 3.88 us  [to_mate_of(): lax.ppermute(array, ('section', 'expert'), [(s * lanes + i, s * lanes + (...]
    ppermute x9 -> x8, starting transfers between devices: 8.45 us -> 7.95 us  [to_mate(): return lax.ppermute(array, 'expert', mates)]
  transfers between devices with their start and end apart: 25 -> 26, of which waited for: 20 -> 19; matrix products, arithmetic and copies ran while one was open for 3% -> 2% of each run, Pallas kernels for 13% -> 16%
where the time goes in v2:
time: 295 us; the launch traced here: 294 us
  waiting for transfers between devices  129 us (44%)
  starting transfers between devices  85.5 us (29%)
  Pallas kernels  50.3 us (17%)
  local copies, waits for them, and re-layouts  23.2 us (8%)
  other arithmetic  4.34 us (1%)
    ppermute x8, waiting for transfers between devices, to_mate(): return lax.ppermute(array, 'expert', mates)  57.7 us
    all_to_all x8, starting transfers between devices, across(): lax.all_to_all(array, 'expert', 0, 0, axis_index_groups=sides, tiled=True)  42.3 us
    ppermute x8, waiting for transfers between devices, to_section(): lax.ppermute(array, ('section', 'expert'), [(s * lanes + i, (s + by) % se...  39.2 us
    ppermute x8, starting transfers between devices, to_section(): lax.ppermute(array, ('section', 'expert'), [(s * lanes + i, (s + by) % se...  31.3 us
    pallas_call x4, Pallas kernels, hidden(): pl.pallas_call(hidden_kernel, grid=(width // block,), in_specs=[pl.BlockS...  27.4 us
    all_to_all x8, waiting for transfers between devices, across(): lax.all_to_all(array, 'expert', 0, 0, axis_index_groups=sides, tiled=True)  26.2 us
    unnamed x48, local copies, waits for them, and re-layouts  17.1 us
    pallas_call x4, Pallas kernels, down(): pl.pallas_call(down_kernel, grid=(width // block,), in_specs=[whole, whol...  10.8 us
  transfers between devices with their start and end apart: 26, of which 19 were waited for; matrix products, arithmetic and copies ran while one was open for 2% of the time, Pallas kernels for 16%

profile of v2, /device:TPU:73, one launch (start us, length us, event | category | flops | bytes accessed | tf_op | source)
XLA Modules:
  0.0 293.8 jit_solution(4535819135691735545)
XLA Ops:
  4.1 3.2 %collective-permute-start.1 = (bf16[64,3584]{1,0:T(8,128)(2,1)}, bf16[64,3584]{1,0:T(8,128)(2,1)S(1)}, u32[]{:S(2)}, u32[]{:S(2)}) collective-permute-start(bf16[64,3584]{1,0:T(8,128)(2,1)} %bitcast.83), channel_id=1, source_target_pairs={{16,17},{17,16},{18,19},{19,18},{20,21},{21,20},{22,23},{23,22},{2... | collective-permute-start | bytes 1376264 | tf_op jit(solution)/shard_map/ppermute | solution.py:179
  8.1 6.3 %collective-permute-done.1.refs_0_ = bf16[64,3584]{1,0:T(8,128)(2,1)S(1)} collective-permute-done((bf16[64,3584]{1,0:T(8,128)(2,1)}, bf16[64,3584]{1,0:T(8,128)(2,1)S(1)}, u32[]{:S(2)}, u32[]{:S(2)}) %collective-permute-start.1) | collective-permute-done | bytes 458784 | tf_op jit(solution)/shard_map/ppermute | solution.py:179
  15.6 2.7 shard_map.122
  18.2 6.4 %all-to-all-start = ((bf16[8,48,3584]{2,1,0:T(8,128)(2,1)}), bf16[8,48,3584]{2,1,0:T(8,128)(2,1)}, u32[]{:S(2)}, u32[]{:S(2)}) async-start(bf16[8,48,3584]{2,1,0:T(8,128)(2,1)} %bitcast.26), calls=%async_computation | async-start | bytes 5505024 | tf_op jit(solution)/shard_map/all_to_all | solution.py:230
  24.6 2.4 dynamic-slice_bitcast_fusion
  27.8 7.1 %collective-permute-done.3.refs_0_ = bf16[64,3584]{1,0:T(8,128)(2,1)S(1)} collective-permute-done((bf16[64,3584]{1,0:T(8,128)(2,1)S(1)}, bf16[64,3584]{1,0:T(8,128)(2,1)S(1)}, u32[]{:S(2)}, u32[]{:S(2)}) %collective-permute-start.3) | collective-permute-done | bytes 458784 | tf_op jit(solution)/shard_map/ppermute | solution.py:176
  37.5 1.6 copy-done.4
  39.1 18.3 %collective-permute-done.4.refs_0_ = bf16[304,1792]{1,0:T(8,128)(2,1)S(1)} collective-permute-done((bf16[304,1792]{1,0:T(8,128)(2,1)S(1)}, bf16[304,1792]{1,0:T(8,128)(2,1)S(1)}, u32[]{:S(2)}, u32[]{:S(2)}) %collective-permute-start.4) | collective-permute-done | bytes 1089568 | tf_op jit(solution)/shard_map/ppermute | solution.py:176
  57.5 4.5 %all-to-all-start.1 = ((bf16[8,48,3584]{2,1,0:T(8,128)(2,1)}), bf16[8,48,3584]{2,1,0:T(8,128)(2,1)}, u32[]{:S(2)}, u32[]{:S(2)}) async-start(bf16[8,48,3584]{2,1,0:T(8,128)(2,1)} %bitcast.75), calls=%async_computation.1 | async-start | bytes 5505024 | tf_op jit(solution)/shard_map/all_to_all | solution.py:230
  63.2 2.3 collective-permute-start.6
  65.5 6.8 %shard_map.124.own_ref = bf16[384,512]{1,0:T(8,128)(2,1)} custom-call(bf16[384,3584]{1,0:T(8,128)(2,1)} %bitcast.27.rows_ref, bf16[3584,512]{1,0:T(8,128)(2,1)} %bitcast.89, bf16[3584,512]{1,0:T(8,128)(2,1)} %bitcast.93), custom_call_target="tpu_custom_call" | custom-call | flops 2818572288 | bytes 10485760 | tf_op jit(solution)/shard_map/pallas_call | solution.py:78
  72.3 3.1 %collective-permute-done.6.refs_1_ = bf16[208,1792]{1,0:T(8,128)(2,1)S(1)} collective-permute-done((bf16[208,1792]{1,0:T(8,128)(2,1)S(1)}, bf16[208,1792]{1,0:T(8,128)(2,1)S(1)}, u32[]{:S(2)}, u32[]{:S(2)}) %collective-permute-start.6) | collective-permute-done | bytes 745504 | tf_op jit(solution)/shard_map/ppermute | solution.py:176
  75.4 8.4 %collective-permute-done.5.mate_ref = bf16[384,512]{1,0:T(8,128)(2,1)S(1)} collective-permute-done((bf16[384,512]{1,0:T(8,128)(2,1)}, bf16[384,512]{1,0:T(8,128)(2,1)S(1)}, u32[]{:S(2)}, u32[]{:S(2)}) %collective-permute-start.5) | collective-permute-done | bytes 393248 | tf_op jit(solution)/shard_map/ppermute | solution.py:176
  84.8 2.7 shard_map.125
  89.8 5.3 %all-to-all-start.2 = ((bf16[8,48,1792]{2,1,0:T(8,128)(2,1)}), bf16[8,48,1792]{2,1,0:T(8,128)(2,1)}, u32[]{:S(2)}, u32[]{:S(2)}) async-start(bf16[8,48,1792]{2,1,0:T(8,128)(2,1)} %bitcast.82), calls=%async_computation.2 | async-start | bytes 2752512 | tf_op jit(solution)/shard_map/all_to_all | solution.py:230
  95.2 6.9 %shard_map.126.own_ref = bf16[384,512]{1,0:T(8,128)(2,1)} custom-call(bf16[384,3584]{1,0:T(8,128)(2,1)} %bitcast.32.rows_ref, bf16[3584,512]{1,0:T(8,128)(2,1)} %bitcast.90, bf16[3584,512]{1,0:T(8,128)(2,1)} %bitcast.94), custom_call_target="tpu_custom_call" | custom-call | flops 2818572288 | bytes 10485760 | tf_op jit(solution)/shard_map/pallas_call | solution.py:78
  102.1 2.3 collective-permute-start.7
  104.4 5.8 %collective-permute-done.7.mate_ref = bf16[384,512]{1,0:T(8,128)(2,1)S(1)} collective-permute-done((bf16[384,512]{1,0:T(8,128)(2,1)}, bf16[384,512]{1,0:T(8,128)(2,1)S(1)}, u32[]{:S(2)}, u32[]{:S(2)}) %collective-permute-start.7) | collective-permute-done | bytes 393248 | tf_op jit(solution)/shard_map/ppermute | solution.py:176
  111.1 2.7 shard_map.127
  115.0 5.6 %all-to-all-start.3 = ((bf16[8,48,1792]{2,1,0:T(8,128)(2,1)}), bf16[8,48,1792]{2,1,0:T(8,128)(2,1)}, u32[]{:S(2)}, u32[]{:S(2)}) async-start(bf16[8,48,1792]{2,1,0:T(8,128)(2,1)} %bitcast.80), calls=%async_computation.3 | async-start | bytes 2752512 | tf_op jit(solution)/shard_map/all_to_all | solution.py:230
  121.9 1.8 shard_map.128
  123.7 12.7 %collective-permute-start.9 = (bf16[128,1792]{1,0:T(8,128)(2,1)S(1)}, bf16[128,1792]{1,0:T(8,128)(2,1)S(1)}, u32[]{:S(2)}, u32[]{:S(2)}) collective-permute-start(bf16[128,1792]{1,0:T(8,128)(2,1)S(1)} %shard_map.128), channel_id=1, source_target_pairs={{0,17},{1,16},{2,19},{3,18},{4,21},{5,20},{6,23},{7,22},{8,25},{9,... | collective-permute-start | bytes 1376264 | tf_op jit(solution)/shard_map/ppermute | solution.py:187
  136.4 9.7 %collective-permute-done.9.far_ref = bf16[128,1792]{1,0:T(8,128)(2,1)S(1)} collective-permute-done((bf16[128,1792]{1,0:T(8,128)(2,1)S(1)}, bf16[128,1792]{1,0:T(8,128)(2,1)S(1)}, u32[]{:S(2)}, u32[]{:S(2)}) %collective-permute-start.9) | collective-permute-done | bytes 458784 | tf_op jit(solution)/shard_map/ppermute | solution.py:187
  148.0 1.5 copy-done.5
  150.3 6.0 %all-to-all-start.4 = ((bf16[8,48,3584]{2,1,0:T(8,128)(2,1)}), bf16[8,48,3584]{2,1,0:T(8,128)(2,1)}, u32[]{:S(2)}, u32[]{:S(2)}) async-start(bf16[8,48,3584]{2,1,0:T(8,128)(2,1)} %bitcast.76), calls=%async_computation.4 | async-start | bytes 5505024 | tf_op jit(solution)/shard_map/all_to_all | solution.py:230
  156.6 1.8 shard_map.130
  159.7 9.3 %collective-permute-done.11.far_ref = bf16[128,1792]{1,0:T(8,128)(2,1)S(1)} collective-permute-done((bf16[128,1792]{1,0:T(8,128)(2,1)S(1)}, bf16[128,1792]{1,0:T(8,128)(2,1)S(1)}, u32[]{:S(2)}, u32[]{:S(2)}) %collective-permute-start.11) | collective-permute-done | bytes 458784 | tf_op jit(solution)/shard_map/ppermute | solution.py:187
  169.0 3.7 %collective-permute-done.10.near_ref.state_ref = bf16[128,1792]{1,0:T(8,128)(2,1)S(1)} collective-permute-done((bf16[128,1792]{1,0:T(8,128)(2,1)S(1)}, bf16[128,1792]{1,0:T(8,128)(2,1)S(1)}, u32[]{:S(2)}, u32[]{:S(2)}) %collective-permute-start.10) | collective-permute-done | bytes 458784 | tf_op jit(solution)/shard_map/ppermute | solution.py:187
  174.0 1.6 copy-done.6
  175.6 14.1 %all-to-all-done.4 = bf16[8,48,3584]{2,1,0:T(8,128)(2,1)} async-done(((bf16[8,48,3584]{2,1,0:T(8,128)(2,1)}), bf16[8,48,3584]{2,1,0:T(8,128)(2,1)}, u32[]{:S(2)}, u32[]{:S(2)}) %all-to-all-start.4) | async-done | bytes 2752544 | tf_op jit(solution)/shard_map/all_to_all | solution.py:230
  189.6 4.4 %all-to-all-start.5 = ((bf16[8,48,3584]{2,1,0:T(8,128)(2,1)}), bf16[8,48,3584]{2,1,0:T(8,128)(2,1)}, u32[]{:S(2)}, u32[]{:S(2)}) async-start(bf16[8,48,3584]{2,1,0:T(8,128)(2,1)} %bitcast.77), calls=%async_computation.5 | async-start | bytes 5505024 | tf_op jit(solution)/shard_map/all_to_all | solution.py:230
  194.1 6.9 %shard_map.132.own_ref = bf16[384,512]{1,0:T(8,128)(2,1)} custom-call(bf16[384,3584]{1,0:T(8,128)(2,1)} %bitcast.40.rows_ref, bf16[3584,512]{1,0:T(8,128)(2,1)} %bitcast.91, bf16[3584,512]{1,0:T(8,128)(2,1)} %bitcast.95), custom_call_target="tpu_custom_call" | custom-call | flops 2818572288 | bytes 10485760 | tf_op jit(solution)/shard_map/pallas_call | solution.py:78
  201.3 8.5 %collective-permute-done.12.mate_ref = bf16[384,512]{1,0:T(8,128)(2,1)S(1)} collective-permute-done((bf16[384,512]{1,0:T(8,128)(2,1)}, bf16[384,512]{1,0:T(8,128)(2,1)S(1)}, u32[]{:S(2)}, u32[]{:S(2)}) %collective-permute-start.12) | collective-permute-done | bytes 393248 | tf_op jit(solution)/shard_map/ppermute | solution.py:176
  210.8 2.7 shard_map.133
  214.6 11.8 %all-to-all-done.5 = bf16[8,48,3584]{2,1,0:T(8,128)(2,1)} async-done(((bf16[8,48,3584]{2,1,0:T(8,128)(2,1)}), bf16[8,48,3584]{2,1,0:T(8,128)(2,1)}, u32[]{:S(2)}, u32[]{:S(2)}) %all-to-all-start.5) | async-done | bytes 2752544 | tf_op jit(solution)/shard_map/all_to_all | solution.py:230
  226.4 4.3 %all-to-all-start.6 = ((bf16[8,48,1792]{2,1,0:T(8,128)(2,1)}), bf16[8,48,1792]{2,1,0:T(8,128)(2,1)}, u32[]{:S(2)}, u32[]{:S(2)}) async-start(bf16[8,48,1792]{2,1,0:T(8,128)(2,1)} %bitcast.81), calls=%async_computation.6 | async-start | bytes 2752512 | tf_op jit(solution)/shard_map/all_to_all | solution.py:230
  230.7 6.9 %shard_map.134.own_ref = bf16[384,512]{1,0:T(8,128)(2,1)} custom-call(bf16[384,3584]{1,0:T(8,128)(2,1)} %bitcast.42.rows_ref, bf16[3584,512]{1,0:T(8,128)(2,1)} %bitcast.92, bf16[3584,512]{1,0:T(8,128)(2,1)} %bitcast.96), custom_call_target="tpu_custom_call" | custom-call | flops 2818572288 | bytes 10485760 | tf_op jit(solution)/shard_map/pallas_call | solution.py:78
  239.1 6.5 %collective-permute-done.13.mate_ref = bf16[384,512]{1,0:T(8,128)(2,1)S(1)} collective-permute-done((bf16[384,512]{1,0:T(8,128)(2,1)}, bf16[384,512]{1,0:T(8,128)(2,1)S(1)}, u32[]{:S(2)}, u32[]{:S(2)}) %collective-permute-start.13) | collective-permute-done | bytes 393248 | tf_op jit(solution)/shard_map/ppermute | solution.py:176
  246.6 2.7 shard_map.135
  250.5 5.7 %all-to-all-start.7 = ((bf16[8,48,1792]{2,1,0:T(8,128)(2,1)}), bf16[8,48,1792]{2,1,0:T(8,128)(2,1)S(1)}, u32[]{:S(2)}, u32[]{:S(2)}) async-start(bf16[8,48,1792]{2,1,0:T(8,128)(2,1)} %bitcast.78), calls=%async_computation.7 | async-start | bytes 2752512 | tf_op jit(solution)/shard_map/all_to_all | solution.py:230
  256.4 1.8 shard_map.136
  258.2 9.5 %collective-permute-start.14 = (bf16[64,1792]{1,0:T(8,128)(2,1)S(1)}, bf16[64,1792]{1,0:T(8,128)(2,1)S(1)}, u32[]{:S(2)}, u32[]{:S(2)}) collective-permute-start(bf16[64,1792]{1,0:T(8,128)(2,1)S(1)} %get-tuple-element.80), channel_id=1, source_target_pairs={{0,16},{1,17},{2,18},{3,19},{4,20},{5,21},{6,22},{7,23},{8,24},{9,... | collective-permute-start | bytes 688136 | tf_op jit(solution)/shard_map/ppermute | solution.py:187
  267.8 1.9 collective-permute-start.15
  270.7 3.1 %collective-permute-done.15 = bf16[64,1792]{1,0:T(8,128)(2,1)S(1)} collective-permute-done((bf16[64,1792]{1,0:T(8,128)(2,1)S(1)}, bf16[64,1792]{1,0:T(8,128)(2,1)S(1)}, u32[]{:S(2)}, u32[]{:S(2)}) %collective-permute-start.15) | collective-permute-done | bytes 229408 | tf_op jit(solution)/shard_map/ppermute | solution.py:187
  274.4 2.9 collective-permute-start.16
  277.3 3.0 %collective-permute-start.17 = (bf16[64,1792]{1,0:T(8,128)(2,1)S(1)}, bf16[64,1792]{1,0:T(8,128)(2,1)S(1)}, u32[]{:S(2)}, u32[]{:S(2)}) collective-permute-start(bf16[64,1792]{1,0:T(8,128)(2,1)S(1)} %get-tuple-element.77), channel_id=1, source_target_pairs={{0,241},{1,240},{2,243},{3,242},{4,245},{5,244},{6,247},{7,246},{8... | collective-permute-start | bytes 688136 | tf_op jit(solution)/shard_map/ppermute | solution.py:187
  281.0 6.6 %collective-permute-done.16 = bf16[64,1792]{1,0:T(8,128)(2,1)S(1)} collective-permute-done((bf16[64,1792]{1,0:T(8,128)(2,1)S(1)}, bf16[64,1792]{1,0:T(8,128)(2,1)S(1)}, u32[]{:S(2)}, u32[]{:S(2)}) %collective-permute-start.16) | collective-permute-done | bytes 229408 | tf_op jit(solution)/shard_map/ppermute | solution.py:187
  287.6 5.3 %collective-permute-done.17 = bf16[64,1792]{1,0:T(8,128)(2,1)S(1)} collective-permute-done((bf16[64,1792]{1,0:T(8,128)(2,1)S(1)}, bf16[64,1792]{1,0:T(8,128)(2,1)S(1)}, u32[]{:S(2)}, u32[]{:S(2)}) %collective-permute-start.17) | collective-permute-done | bytes 229408 | tf_op jit(solution)/shard_map/ppermute | solution.py:187
  (116 shorter events, 31.6 us)
Async XLA Ops:
  3.8 3.5 %collective-permute-start = (f32[8,64]{1,0:T(8,128)S(1)}, f32[8,64]{1,0:T(8,128)S(1)}, u32[]{:S(2)}, u32[]{:S(2)}) collective-permute-start(f32[8,64]{1,0:T(8,128)S(1)} %stack.7), channel_id=1, source_target_pairs={{0,1},{1,0},{2,3},{3,2},{4,5},{5,4},{6,7},{7,6},{8,9},{9,8},{10,11... | collective-permute-start | bytes 6152 | tf_op jit(solution)/shard_map/ppermute | solution.py:176
  4.1 10.3 %collective-permute-start.1 = (bf16[64,3584]{1,0:T(8,128)(2,1)}, bf16[64,3584]{1,0:T(8,128)(2,1)S(1)}, u32[]{:S(2)}, u32[]{:S(2)}) collective-permute-start(bf16[64,3584]{1,0:T(8,128)(2,1)} %bitcast.83), channel_id=1, source_target_pairs={{16,17},{17,16},{18,19},{19,18},{20,21},{21,20},{22,23},{23,22},{2... | collective-permute-start | bytes 1376264 | tf_op jit(solution)/shard_map/ppermute | solution.py:179
  7.3 7.1 %collective-permute-start.2 = (bf16[64,3584]{1,0:T(8,128)(2,1)}, bf16[64,3584]{1,0:T(8,128)(2,1)S(1)}, u32[]{:S(2)}, u32[]{:S(2)}) collective-permute-start(bf16[64,3584]{1,0:T(8,128)(2,1)} %bitcast.84), channel_id=1, source_target_pairs={{0,1},{1,0},{2,3},{3,2},{4,5},{5,4},{6,7},{7,6},{8,9},{9,8},{10,11... | collective-permute-start | bytes 1376264 | tf_op jit(solution)/shard_map/ppermute | solution.py:179
  14.4 3.9 %copy-start.20 = (bf16[64,3584]{1,0:T(8,128)(2,1)}, bf16[64,3584]{1,0:T(8,128)(2,1)S(1)}, u32[]{:S(2)}) copy-start(bf16[64,3584]{1,0:T(8,128)(2,1)S(1)} %collective-permute-done.2.refs_1_) | copy-start | bytes 1376260
  14.4 1.2 copy-start.18
  18.2 39.2 %all-to-all-start = ((bf16[8,48,3584]{2,1,0:T(8,128)(2,1)}), bf16[8,48,3584]{2,1,0:T(8,128)(2,1)}, u32[]{:S(2)}, u32[]{:S(2)}) async-start(bf16[8,48,3584]{2,1,0:T(8,128)(2,1)} %bitcast.26), calls=%async_computation | async-start | bytes 5505024 | tf_op jit(solution)/shard_map/all_to_all | solution.py:230
  24.6 2.4 copy-start.22
  24.6 3.0 %copy-start.19 = (bf16[1,64,3584]{2,1,0:T(8,128)(2,1)S(1)}, bf16[1,64,3584]{2,1,0:T(8,128)(2,1)}, u32[]{:S(2)}) copy-start(bf16[1,64,3584]{2,1,0:T(8,128)(2,1)} %param.11) | copy-start | bytes 1376260
  27.0 8.6 %copy-start.23 = (bf16[512,1792]{1,0:T(8,128)(2,1)}, bf16[512,1792]{1,0:T(8,128)(2,1)S(1)}, u32[]{:S(2)}) copy-start(bf16[512,1792]{1,0:T(8,128)(2,1)S(1)} %get-tuple-element.49) | copy-start | bytes 5505028
  27.0 8.5 %copy-start.21 = (bf16[64,3584]{1,0:T(8,128)(2,1)S(1)}, bf16[64,3584]{1,0:T(8,128)(2,1)}, u32[]{:S(2)}) copy-start(bf16[64,3584]{1,0:T(8,128)(2,1)} %copy-done.20) | copy-start | bytes 1376260
  27.1 7.8 %collective-permute-start.3 = (bf16[64,3584]{1,0:T(8,128)(2,1)S(1)}, bf16[64,3584]{1,0:T(8,128)(2,1)S(1)}, u32[]{:S(2)}, u32[]{:S(2)}) collective-permute-start(bf16[64,3584]{1,0:T(8,128)(2,1)S(1)} %bitcast.86), channel_id=1, source_target_pairs={{0,1},{1,0},{2,3},{3,2},{4,5},{5,4},{6,7},{7,6},{8,9},{9,8},{10,11... | collective-permute-start | bytes 1376264 | tf_op jit(solution)/shard_map/ppermute | solution.py:176
  34.9 22.5 %collective-permute-start.4 = (bf16[304,1792]{1,0:T(8,128)(2,1)S(1)}, bf16[304,1792]{1,0:T(8,128)(2,1)S(1)}, u32[]{:S(2)}, u32[]{:S(2)}) collective-permute-start(bf16[304,1792]{1,0:T(8,128)(2,1)S(1)} %slice.79), channel_id=1, source_target_pairs={{0,1},{1,0},{2,3},{3,2},{4,5},{5,4},{6,7},{7,6},{8,9},{9,8},{10,11... | collective-permute-start | bytes 3268616 | tf_op jit(solution)/shard_map/ppermute | solution.py:176
  37.5 1.6 copy-start.4
  57.5 32.4 %all-to-all-start.1 = ((bf16[8,48,3584]{2,1,0:T(8,128)(2,1)}), bf16[8,48,3584]{2,1,0:T(8,128)(2,1)}, u32[]{:S(2)}, u32[]{:S(2)}) async-start(bf16[8,48,3584]{2,1,0:T(8,128)(2,1)} %bitcast.75), calls=%async_computation.1 | async-start | bytes 5505024 | tf_op jit(solution)/shard_map/all_to_all | solution.py:230
  63.2 12.2 %collective-permute-start.6 = (bf16[208,1792]{1,0:T(8,128)(2,1)S(1)}, bf16[208,1792]{1,0:T(8,128)(2,1)S(1)}, u32[]{:S(2)}, u32[]{:S(2)}) collective-permute-start(bf16[208,1792]{1,0:T(8,128)(2,1)S(1)} %slice.87), channel_id=1, source_target_pairs={{0,1},{1,0},{2,3},{3,2},{4,5},{5,4},{6,7},{7,6},{8,9},{9,8},{10,11... | collective-permute-start | bytes 2236424 | tf_op jit(solution)/shard_map/ppermute | solution.py:176
  72.3 11.5 %collective-permute-start.5 = (bf16[384,512]{1,0:T(8,128)(2,1)}, bf16[384,512]{1,0:T(8,128)(2,1)S(1)}, u32[]{:S(2)}, u32[]{:S(2)}) collective-permute-start(bf16[384,512]{1,0:T(8,128)(2,1)} %shard_map.124.own_ref), channel_id=1, source_target_pairs={{0,1},{1,0},{2,3},{3,2},{4,5},{5,4},{6,7},{7,6},{8,9},{9,8},{10,11... | collective-permute-start | bytes 1179656 | tf_op jit(solution)/shard_map/ppermute | solution.py:176
  83.8 1.0 copy-start.14
  88.4 1.1 copy-start.10
  89.8 25.2 %all-to-all-start.2 = ((bf16[8,48,1792]{2,1,0:T(8,128)(2,1)}), bf16[8,48,1792]{2,1,0:T(8,128)(2,1)}, u32[]{:S(2)}, u32[]{:S(2)}) async-start(bf16[8,48,1792]{2,1,0:T(8,128)(2,1)} %bitcast.82), calls=%async_computation.2 | async-start | bytes 2752512 | tf_op jit(solution)/shard_map/all_to_all | solution.py:230
  95.2 14.9 %copy-start.1 = (bf16[208,1792]{1,0:T(8,128)(2,1)S(1)}, bf16[208,1792]{1,0:T(8,128)(2,1)}, u32[]{:S(2)}) copy-start(bf16[208,1792]{1,0:T(8,128)(2,1)} %copy-done) | copy-start | bytes 2236420
  102.1 8.1 %collective-permute-start.7 = (bf16[384,512]{1,0:T(8,128)(2,1)}, bf16[384,512]{1,0:T(8,128)(2,1)S(1)}, u32[]{:S(2)}, u32[]{:S(2)}) collective-permute-start(bf16[384,512]{1,0:T(8,128)(2,1)} %shard_map.126.own_ref), channel_id=1, source_target_pairs={{0,1},{1,0},{2,3},{3,2},{4,5},{5,4},{6,7},{7,6},{8,9},{9,8},{10,11... | collective-permute-start | bytes 1179656 | tf_op jit(solution)/shard_map/ppermute | solution.py:176
  110.1 1.0 copy-start.16
  113.8 1.2 copy-start.8
  115.0 35.3 %all-to-all-start.3 = ((bf16[8,48,1792]{2,1,0:T(8,128)(2,1)}), bf16[8,48,1792]{2,1,0:T(8,128)(2,1)}, u32[]{:S(2)}, u32[]{:S(2)}) async-start(bf16[8,48,1792]{2,1,0:T(8,128)(2,1)} %bitcast.80), calls=%async_computation.3 | async-start | bytes 2752512 | tf_op jit(solution)/shard_map/all_to_all | solution.py:230
  120.9 1.0 copy-start.11
  123.7 22.4 %collective-permute-start.9 = (bf16[128,1792]{1,0:T(8,128)(2,1)S(1)}, bf16[128,1792]{1,0:T(8,128)(2,1)S(1)}, u32[]{:S(2)}, u32[]{:S(2)}) collective-permute-start(bf16[128,1792]{1,0:T(8,128)(2,1)S(1)} %shard_map.128), channel_id=1, source_target_pairs={{0,17},{1,16},{2,19},{3,18},{4,21},{5,20},{6,23},{7,22},{8,25},{9,... | collective-permute-start | bytes 1376264 | tf_op jit(solution)/shard_map/ppermute | solution.py:187
  136.4 10.4 %collective-permute-start.8 = (bf16[128,1792]{1,0:T(8,128)(2,1)S(1)}, bf16[128,1792]{1,0:T(8,128)(2,1)S(1)}, u32[]{:S(2)}, u32[]{:S(2)}) collective-permute-start(bf16[128,1792]{1,0:T(8,128)(2,1)S(1)} %shard_map.128), channel_id=1, source_target_pairs={{0,16},{1,17},{2,18},{3,19},{4,20},{5,21},{6,22},{7,23},{8,24},{9,... | collective-permute-start | bytes 1376264 | tf_op jit(solution)/shard_map/ppermute | solution.py:187
  148.0 1.6 copy-start.5
  150.3 39.3 %all-to-all-start.4 = ((bf16[8,48,3584]{2,1,0:T(8,128)(2,1)}), bf16[8,48,3584]{2,1,0:T(8,128)(2,1)}, u32[]{:S(2)}, u32[]{:S(2)}) async-start(bf16[8,48,3584]{2,1,0:T(8,128)(2,1)} %bitcast.76), calls=%async_computation.4 | async-start | bytes 5505024 | tf_op jit(solution)/shard_map/all_to_all | solution.py:230
  158.4 10.7 %collective-permute-start.11 = (bf16[128,1792]{1,0:T(8,128)(2,1)S(1)}, bf16[128,1792]{1,0:T(8,128)(2,1)S(1)}, u32[]{:S(2)}, u32[]{:S(2)}) collective-permute-start(bf16[128,1792]{1,0:T(8,128)(2,1)S(1)} %shard_map.130), channel_id=1, source_target_pairs={{0,241},{1,240},{2,243},{3,242},{4,245},{5,244},{6,247},{7,246},{8... | collective-permute-start | bytes 1376264 | tf_op jit(solution)/shard_map/ppermute | solution.py:187
  158.7 14.0 %collective-permute-start.10 = (bf16[128,1792]{1,0:T(8,128)(2,1)S(1)}, bf16[128,1792]{1,0:T(8,128)(2,1)S(1)}, u32[]{:S(2)}, u32[]{:S(2)}) collective-permute-start(bf16[128,1792]{1,0:T(8,128)(2,1)S(1)} %shard_map.130), channel_id=1, source_target_pairs={{0,240},{1,241},{2,242},{3,243},{4,244},{5,245},{6,246},{7,247},{8... | collective-permute-start | bytes 1376264 | tf_op jit(solution)/shard_map/ppermute | solution.py:187
  174.0 1.6 copy-start.6
  189.6 36.7 %all-to-all-start.5 = ((bf16[8,48,3584]{2,1,0:T(8,128)(2,1)}), bf16[8,48,3584]{2,1,0:T(8,128)(2,1)}, u32[]{:S(2)}, u32[]{:S(2)}) async-start(bf16[8,48,3584]{2,1,0:T(8,128)(2,1)} %bitcast.77), calls=%async_computation.5 | async-start | bytes 5505024 | tf_op jit(solution)/shard_map/all_to_all | solution.py:230
  194.1 15.7 %copy-start.2 = (bf16[208,1792]{1,0:T(8,128)(2,1)S(1)}, bf16[208,1792]{1,0:T(8,128)(2,1)}, u32[]{:S(2)}) copy-start(bf16[208,1792]{1,0:T(8,128)(2,1)} %copy-done) | copy-start | bytes 2236420
  201.0 8.8 %collective-permute-start.12 = (bf16[384,512]{1,0:T(8,128)(2,1)}, bf16[384,512]{1,0:T(8,128)(2,1)S(1)}, u32[]{:S(2)}, u32[]{:S(2)}) collective-permute-start(bf16[384,512]{1,0:T(8,128)(2,1)} %shard_map.132.own_ref), channel_id=1, source_target_pairs={{0,1},{1,0},{2,3},{3,2},{4,5},{5,4},{6,7},{7,6},{8,9},{9,8},{10,11... | collective-permute-start | bytes 1179656 | tf_op jit(solution)/shard_map/ppermute | solution.py:176
  209.8 1.0 copy-start.17
  213.5 1.1 copy-start.9
  226.4 24.1 %all-to-all-start.6 = ((bf16[8,48,1792]{2,1,0:T(8,128)(2,1)}), bf16[8,48,1792]{2,1,0:T(8,128)(2,1)}, u32[]{:S(2)}, u32[]{:S(2)}) async-start(bf16[8,48,1792]{2,1,0:T(8,128)(2,1)} %bitcast.81), calls=%async_computation.6 | async-start | bytes 2752512 | tf_op jit(solution)/shard_map/all_to_all | solution.py:230
  230.7 15.0 %copy-start.3 = (bf16[208,1792]{1,0:T(8,128)(2,1)S(1)}, bf16[208,1792]{1,0:T(8,128)(2,1)}, u32[]{:S(2)}) copy-start(bf16[208,1792]{1,0:T(8,128)(2,1)} %copy-done) | copy-start | bytes 2236420
  237.6 8.1 %collective-permute-start.13 = (bf16[384,512]{1,0:T(8,128)(2,1)}, bf16[384,512]{1,0:T(8,128)(2,1)S(1)}, u32[]{:S(2)}, u32[]{:S(2)}) collective-permute-start(bf16[384,512]{1,0:T(8,128)(2,1)} %shard_map.134.own_ref), channel_id=1, source_target_pairs={{0,1},{1,0},{2,3},{3,2},{4,5},{5,4},{6,7},{7,6},{8,9},{9,8},{10,11... | collective-permute-start | bytes 1179656 | tf_op jit(solution)/shard_map/ppermute | solution.py:176
  245.6 1.0 copy-start.15
  249.4 1.1 copy-start.7
  250.5 5.9 %copy-start.13 = (bf16[128,1792]{1,0:T(8,128)(2,1)S(1)}, bf16[128,1792]{1,0:T(8,128)(2,1)}, u32[]{:S(2)}) copy-start(bf16[128,1792]{1,0:T(8,128)(2,1)} %copy-done.12) | copy-start | bytes 1376260
  250.5 23.4 %all-to-all-start.7 = ((bf16[8,48,1792]{2,1,0:T(8,128)(2,1)}), bf16[8,48,1792]{2,1,0:T(8,128)(2,1)S(1)}, u32[]{:S(2)}, u32[]{:S(2)}) async-start(bf16[8,48,1792]{2,1,0:T(8,128)(2,1)} %bitcast.78), calls=%async_computation.7 | async-start | bytes 2752512 | tf_op jit(solution)/shard_map/all_to_all | solution.py:230
  258.2 12.5 %collective-permute-start.14 = (bf16[64,1792]{1,0:T(8,128)(2,1)S(1)}, bf16[64,1792]{1,0:T(8,128)(2,1)S(1)}, u32[]{:S(2)}, u32[]{:S(2)}) collective-permute-start(bf16[64,1792]{1,0:T(8,128)(2,1)S(1)} %get-tuple-element.80), channel_id=1, source_target_pairs={{0,16},{1,17},{2,18},{3,19},{4,20},{5,21},{6,22},{7,23},{8,24},{9,... | collective-permute-start | bytes 688136 | tf_op jit(solution)/shard_map/ppermute | solution.py:187
  267.8 6.0 %collective-permute-start.15 = (bf16[64,1792]{1,0:T(8,128)(2,1)S(1)}, bf16[64,1792]{1,0:T(8,128)(2,1)S(1)}, u32[]{:S(2)}, u32[]{:S(2)}) collective-permute-start(bf16[64,1792]{1,0:T(8,128)(2,1)S(1)} %get-tuple-element.81), channel_id=1, source_target_pairs={{0,17},{1,16},{2,19},{3,18},{4,21},{5,20},{6,23},{7,22},{8,25},{9,... | collective-permute-start | bytes 688136 | tf_op jit(solution)/shard_map/ppermute | solution.py:187
  274.4 13.3 %collective-permute-start.16 = (bf16[64,1792]{1,0:T(8,128)(2,1)S(1)}, bf16[64,1792]{1,0:T(8,128)(2,1)S(1)}, u32[]{:S(2)}, u32[]{:S(2)}) collective-permute-start(bf16[64,1792]{1,0:T(8,128)(2,1)S(1)} %get-tuple-element.76), channel_id=1, source_target_pairs={{0,240},{1,241},{2,242},{3,243},{4,244},{5,245},{6,246},{7,247},{8... | collective-permute-start | bytes 688136 | tf_op jit(solution)/shard_map/ppermute | solution.py:187
  277.3 15.7 %collective-permute-start.17 = (bf16[64,1792]{1,0:T(8,128)(2,1)S(1)}, bf16[64,1792]{1,0:T(8,128)(2,1)S(1)}, u32[]{:S(2)}, u32[]{:S(2)}) collective-permute-start(bf16[64,1792]{1,0:T(8,128)(2,1)S(1)} %get-tuple-element.77), channel_id=1, source_target_pairs={{0,241},{1,240},{2,243},{3,242},{4,245},{5,244},{6,247},{7,246},{8... | collective-permute-start | bytes 688136 | tf_op jit(solution)/shard_map/ppermute | solution.py:187
  (2 other events, 1.7 us)

commit v3 on v2

--- a/solution.py
+++ b/solution.py
@@ -166,7 +166,7 @@
     lane = lax.axis_index("expert")
     side = lane % 2
     group = jnp.where((lane % 4 == 0) | (lane % 4 == 3), 0, 1)
-    order = [0, 2, 4, 6, 5, 7, 1, 3]
+    order = [0, 2, 6, 4, 7, 5, 1, 3]
     members = [2 * e if e % 2 == 0 else 2 * e + 1 for e in order]
     sides = [members, [i ^ 1 for i in members]]
     place = [order.index(e) for e in range(experts)]
@@ -205,16 +205,13 @@
         return jnp.sum(ranked + start, axis=1), scale, live.astype(jnp.int32).reshape(1, 1)
 
     plans = [plan(direction, tick) for direction in range(2) for tick in range(tick_count)]
-    own_plan = jnp.stack([p[0].astype(jnp.float32) for p in plans] + [p[1] for p in plans])
-    mate_plan = to_mate(own_plan)
-    late_forward, mate_plan = together(forward_in[0], mate_plan)
-    own_slots = own_plan[: len(plans)].astype(jnp.int32) + side * most_rows
-    mate_slots = mate_plan[: len(plans)].astype(jnp.int32) + (1 - side) * most_rows
-    slots = jnp.concatenate([own_slots, mate_slots], axis=1)
-    scales = jnp.concatenate([own_plan[len(plans) :], mate_plan[len(plans) :]], axis=1)
-    columns = [
-        (slots[at].reshape(-1, 1), scales[at].reshape(-1, 1)) for at in range(len(plans))
-    ]
+    own_slots = jnp.stack([p[0] for p in plans])
+    mate_slots = to_mate(own_slots)
+    late_forward, mate_slots = together(forward_in[0], mate_slots)
+    slots = jnp.concatenate(
+        [own_slots + side * most_rows, mate_slots + (1 - side) * most_rows], axis=1
+    )
+    own_scales = jnp.stack([p[1] for p in plans])
     group_flag = group.astype(jnp.int32).reshape(1, 1)
 
     def pair_slots(direction, tick):
@@ -264,8 +261,12 @@
     forward_mates = [to_mate_of(forward, 1), to_mate_of(late_forward, 0)]
     packed_forward = first_pack(0, forward, *forward_mates)
     forward_mate = forward_mates[0] + forward_mates[1]
-    reverse, packed_forward = together(reverse, packed_forward)
+    reverse, packed_forward, own_scales = together(reverse, packed_forward, own_scales)
     reverse_mate = to_mate(reverse)
+    scales = jnp.concatenate([own_scales, to_mate(own_scales)], axis=1)
+    columns = [
+        (slots[at].reshape(-1, 1), scales[at].reshape(-1, 1)) for at in range(len(plans))
+    ]
     reverse_mate, down_other = together(reverse_mate, down_other)
     down_mate = [to_mate(down_other[:depth])]
     for tick in range(tick_count):

time: 295 us -> 292 us (0.990)
  waiting for transfers between devices: 129 us -> 126 us
    ppermute x8 -> x9, waiting for transfers between devices: 57.7 us -> 56.8 us  [to_mate(): return lax.ppermute(array, 'expert', mates)]
    ppermute x8 -> x9, starting transfers between devices: 7.95 us -> 8.33 us  [to_mate(): return lax.ppermute(array, 'expert', mates)]
    unnamed x48 -> x44, local copies, waits for them, and re-layouts: 17.1 us -> 16.9 us
  transfers between devices with their start and end apart: 26 -> 27, of which waited for: 19 -> 18; matrix products, arithmetic and copies ran while one was open for 2% -> 2% of each run, Pallas kernels for 16% -> 16%
where the time goes in v3:
time: 292 us; the launch traced here: 291 us
  waiting for transfers between devices  126 us (43%)
  starting transfers between devices  86.2 us (30%)
  Pallas kernels  50.2 us (17%)
  local copies, waits for them, and re-layouts  23 us (8%)
  other arithmetic  4.32 us (1%)
    ppermute x9, waiting for transfers between devices, to_mate(): return lax.ppermute(array, 'expert', mates)  56.8 us
    all_to_all x8, starting transfers between devices, across(): lax.all_to_all(array, 'expert', 0, 0, axis_index_groups=sides, tiled=True)  43.2 us
    ppermute x8, waiting for transfers between devices, to_section(): lax.ppermute(array, ('section', 'expert'), [(s * lanes + i, (s + by) % se...  39.2 us
    ppermute x8, starting transfers between devices, to_section(): lax.ppermute(array, ('section', 'expert'), [(s * lanes + i, (s + by) % se...  30.8 us
    pallas_call x4, Pallas kernels, hidden(): pl.pallas_call(hidden_kernel, grid=(width // block,), in_specs=[pl.BlockS...  27.4 us
    all_to_all x8, waiting for transfers between devices, across(): lax.all_to_all(array, 'expert', 0, 0, axis_index_groups=sides, tiled=True)  24.9 us
    unnamed x44, local copies, waits for them, and re-layouts  16.9 us
    pallas_call x4, Pallas kernels, down(): pl.pallas_call(down_kernel, grid=(width // block,), in_specs=[whole, whol...  10.8 us
  transfers between devices with their start and end apart: 27, of which 18 were waited for; matrix products, arithmetic and copies ran while one was open for 2% of the time, Pallas kernels for 16%

profile of v3, /device:TPU:73, one launch (start us, length us, event | category | flops | bytes accessed | tf_op | source)
XLA Modules:
  0.0 291.3 jit_solution(10719050863921789422)
XLA Ops:
  3.3 3.2 %collective-permute-start.1 = (bf16[64,3584]{1,0:T(8,128)(2,1)}, bf16[64,3584]{1,0:T(8,128)(2,1)S(1)}, u32[]{:S(2)}, u32[]{:S(2)}) collective-permute-start(bf16[64,3584]{1,0:T(8,128)(2,1)} %bitcast.79), channel_id=1, source_target_pairs={{16,17},{17,16},{18,19},{19,18},{20,21},{21,20},{22,23},{23,22},{2... | collective-permute-start | bytes 1376264 | tf_op jit(solution)/shard_map/ppermute | solution.py:179
  8.0 5.6 %collective-permute-done.1.refs_0_ = bf16[64,3584]{1,0:T(8,128)(2,1)S(1)} collective-permute-done((bf16[64,3584]{1,0:T(8,128)(2,1)}, bf16[64,3584]{1,0:T(8,128)(2,1)S(1)}, u32[]{:S(2)}, u32[]{:S(2)}) %collective-permute-start.1) | collective-permute-done | bytes 458784 | tf_op jit(solution)/shard_map/ppermute | solution.py:179
  14.6 2.7 shard_map.122
  17.3 6.4 %all-to-all-start = ((bf16[8,48,3584]{2,1,0:T(8,128)(2,1)}), bf16[8,48,3584]{2,1,0:T(8,128)(2,1)}, u32[]{:S(2)}, u32[]{:S(2)}) async-start(bf16[8,48,3584]{2,1,0:T(8,128)(2,1)} %bitcast.26), calls=%async_computation | async-start | bytes 5505024 | tf_op jit(solution)/shard_map/all_to_all | solution.py:227
  23.7 2.4 dynamic-slice_bitcast_fusion
  27.8 6.1 %collective-permute-done.3.refs_0_ = bf16[64,3584]{1,0:T(8,128)(2,1)S(1)} collective-permute-done((bf16[64,3584]{1,0:T(8,128)(2,1)S(1)}, bf16[64,3584]{1,0:T(8,128)(2,1)S(1)}, u32[]{:S(2)}, u32[]{:S(2)}) %collective-permute-start.3) | collective-permute-done | bytes 458784 | tf_op jit(solution)/shard_map/ppermute | solution.py:176
  36.5 1.6 copy-done.4
  38.2 18.4 %collective-permute-done.4.refs_0_ = bf16[304,1792]{1,0:T(8,128)(2,1)S(1)} collective-permute-done((bf16[304,1792]{1,0:T(8,128)(2,1)S(1)}, bf16[304,1792]{1,0:T(8,128)(2,1)S(1)}, u32[]{:S(2)}, u32[]{:S(2)}) %collective-permute-start.4) | collective-permute-done | bytes 1089568 | tf_op jit(solution)/shard_map/ppermute | solution.py:176
  56.6 4.5 %all-to-all-start.1 = ((bf16[8,48,3584]{2,1,0:T(8,128)(2,1)}), bf16[8,48,3584]{2,1,0:T(8,128)(2,1)}, u32[]{:S(2)}, u32[]{:S(2)}) async-start(bf16[8,48,3584]{2,1,0:T(8,128)(2,1)} %bitcast.71), calls=%async_computation.1 | async-start | bytes 5505024 | tf_op jit(solution)/shard_map/all_to_all | solution.py:227
  62.3 2.3 collective-permute-start.7
  64.6 6.8 %shard_map.124.own_ref = bf16[384,512]{1,0:T(8,128)(2,1)} custom-call(bf16[384,3584]{1,0:T(8,128)(2,1)} %bitcast.27.rows_ref, bf16[3584,512]{1,0:T(8,128)(2,1)} %bitcast.85, bf16[3584,512]{1,0:T(8,128)(2,1)} %bitcast.89), custom_call_target="tpu_custom_call" | custom-call | flops 2818572288 | bytes 10485760 | tf_op jit(solution)/shard_map/pallas_call | solution.py:78
  71.4 3.1 %collective-permute-done.7.refs_1_ = bf16[208,1792]{1,0:T(8,128)(2,1)S(1)} collective-permute-done((bf16[208,1792]{1,0:T(8,128)(2,1)S(1)}, bf16[208,1792]{1,0:T(8,128)(2,1)S(1)}, u32[]{:S(2)}, u32[]{:S(2)}) %collective-permute-start.7) | collective-permute-done | bytes 745504 | tf_op jit(solution)/shard_map/ppermute | solution.py:176
  74.5 8.4 %collective-permute-done.6.mate_ref = bf16[384,512]{1,0:T(8,128)(2,1)S(1)} collective-permute-done((bf16[384,512]{1,0:T(8,128)(2,1)}, bf16[384,512]{1,0:T(8,128)(2,1)S(1)}, u32[]{:S(2)}, u32[]{:S(2)}) %collective-permute-start.6) | collective-permute-done | bytes 393248 | tf_op jit(solution)/shard_map/ppermute | solution.py:176
  83.9 2.7 shard_map.125
  88.7 5.6 %all-to-all-start.2 = ((bf16[8,48,1792]{2,1,0:T(8,128)(2,1)}), bf16[8,48,1792]{2,1,0:T(8,128)(2,1)}, u32[]{:S(2)}, u32[]{:S(2)}) async-start(bf16[8,48,1792]{2,1,0:T(8,128)(2,1)} %bitcast.78), calls=%async_computation.2 | async-start | bytes 2752512 | tf_op jit(solution)/shard_map/all_to_all | solution.py:227
  94.3 6.9 %shard_map.126.own_ref = bf16[384,512]{1,0:T(8,128)(2,1)} custom-call(bf16[384,3584]{1,0:T(8,128)(2,1)} %bitcast.32.rows_ref, bf16[3584,512]{1,0:T(8,128)(2,1)} %bitcast.86, bf16[3584,512]{1,0:T(8,128)(2,1)} %bitcast.90), custom_call_target="tpu_custom_call" | custom-call | flops 2818572288 | bytes 10485760 | tf_op jit(solution)/shard_map/pallas_call | solution.py:78
  101.2 1.6 collective-permute-start.8
  102.8 5.8 %collective-permute-done.8.mate_ref = bf16[384,512]{1,0:T(8,128)(2,1)S(1)} collective-permute-done((bf16[384,512]{1,0:T(8,128)(2,1)}, bf16[384,512]{1,0:T(8,128)(2,1)S(1)}, u32[]{:S(2)}, u32[]{:S(2)}) %collective-permute-start.8) | collective-permute-done | bytes 393248 | tf_op jit(solution)/shard_map/ppermute | solution.py:176
  109.6 2.7 shard_map.127
  113.5 5.7 %all-to-all-start.3 = ((bf16[8,48,1792]{2,1,0:T(8,128)(2,1)}), bf16[8,48,1792]{2,1,0:T(8,128)(2,1)}, u32[]{:S(2)}, u32[]{:S(2)}) async-start(bf16[8,48,1792]{2,1,0:T(8,128)(2,1)} %bitcast.76), calls=%async_computation.3 | async-start | bytes 2752512 | tf_op jit(solution)/shard_map/all_to_all | solution.py:227
  120.5 1.8 shard_map.128
  122.3 13.2 %collective-permute-start.10 = (bf16[128,1792]{1,0:T(8,128)(2,1)S(1)}, bf16[128,1792]{1,0:T(8,128)(2,1)S(1)}, u32[]{:S(2)}, u32[]{:S(2)}) collective-permute-start(bf16[128,1792]{1,0:T(8,128)(2,1)S(1)} %shard_map.128), channel_id=1, source_target_pairs={{0,17},{1,16},{2,19},{3,18},{4,21},{5,20},{6,23},{7,22},{8,25},{9,... | collective-permute-start | bytes 1376264 | tf_op jit(solution)/shard_map/ppermute | solution.py:187
  135.5 9.7 %collective-permute-done.10.far_ref = bf16[128,1792]{1,0:T(8,128)(2,1)S(1)} collective-permute-done((bf16[128,1792]{1,0:T(8,128)(2,1)S(1)}, bf16[128,1792]{1,0:T(8,128)(2,1)S(1)}, u32[]{:S(2)}, u32[]{:S(2)}) %collective-permute-start.10) | collective-permute-done | bytes 458784 | tf_op jit(solution)/shard_map/ppermute | solution.py:187
  147.1 1.5 copy-done.5
  149.4 6.0 %all-to-all-start.4 = ((bf16[8,48,3584]{2,1,0:T(8,128)(2,1)}), bf16[8,48,3584]{2,1,0:T(8,128)(2,1)}, u32[]{:S(2)}, u32[]{:S(2)}) async-start(bf16[8,48,3584]{2,1,0:T(8,128)(2,1)} %bitcast.72), calls=%async_computation.4 | async-start | bytes 5505024 | tf_op jit(solution)/shard_map/all_to_all | solution.py:227
  155.7 1.8 shard_map.130
  158.8 9.3 %collective-permute-done.12.far_ref = bf16[128,1792]{1,0:T(8,128)(2,1)S(1)} collective-permute-done((bf16[128,1792]{1,0:T(8,128)(2,1)S(1)}, bf16[128,1792]{1,0:T(8,128)(2,1)S(1)}, u32[]{:S(2)}, u32[]{:S(2)}) %collective-permute-start.12) | collective-permute-done | bytes 458784 | tf_op jit(solution)/shard_map/ppermute | solution.py:187
  168.1 3.7 %collective-permute-done.11.near_ref.state_ref = bf16[128,1792]{1,0:T(8,128)(2,1)S(1)} collective-permute-done((bf16[128,1792]{1,0:T(8,128)(2,1)S(1)}, bf16[128,1792]{1,0:T(8,128)(2,1)S(1)}, u32[]{:S(2)}, u32[]{:S(2)}) %collective-permute-start.11) | collective-permute-done | bytes 458784 | tf_op jit(solution)/shard_map/ppermute | solution.py:187
  173.1 1.6 copy-done.6
  174.7 13.6 %all-to-all-done.4 = bf16[8,48,3584]{2,1,0:T(8,128)(2,1)} async-done(((bf16[8,48,3584]{2,1,0:T(8,128)(2,1)}), bf16[8,48,3584]{2,1,0:T(8,128)(2,1)}, u32[]{:S(2)}, u32[]{:S(2)}) %all-to-all-start.4) | async-done | bytes 2752544 | tf_op jit(solution)/shard_map/all_to_all | solution.py:227
  188.2 4.4 %all-to-all-start.5 = ((bf16[8,48,3584]{2,1,0:T(8,128)(2,1)}), bf16[8,48,3584]{2,1,0:T(8,128)(2,1)}, u32[]{:S(2)}, u32[]{:S(2)}) async-start(bf16[8,48,3584]{2,1,0:T(8,128)(2,1)} %bitcast.73), calls=%async_computation.5 | async-start | bytes 5505024 | tf_op jit(solution)/shard_map/all_to_all | solution.py:227
  192.7 6.9 %shard_map.132.own_ref = bf16[384,512]{1,0:T(8,128)(2,1)} custom-call(bf16[384,3584]{1,0:T(8,128)(2,1)} %bitcast.40.rows_ref, bf16[3584,512]{1,0:T(8,128)(2,1)} %bitcast.87, bf16[3584,512]{1,0:T(8,128)(2,1)} %bitcast.91), custom_call_target="tpu_custom_call" | custom-call | flops 2818572288 | bytes 10485760 | tf_op jit(solution)/shard_map/pallas_call | solution.py:78
  199.9 8.4 %collective-permute-done.13.mate_ref = bf16[384,512]{1,0:T(8,128)(2,1)S(1)} collective-permute-done((bf16[384,512]{1,0:T(8,128)(2,1)}, bf16[384,512]{1,0:T(8,128)(2,1)S(1)}, u32[]{:S(2)}, u32[]{:S(2)}) %collective-permute-start.13) | collective-permute-done | bytes 393248 | tf_op jit(solution)/shard_map/ppermute | solution.py:176
  209.3 2.7 shard_map.133
  213.1 11.3 %all-to-all-done.5 = bf16[8,48,3584]{2,1,0:T(8,128)(2,1)} async-done(((bf16[8,48,3584]{2,1,0:T(8,128)(2,1)}), bf16[8,48,3584]{2,1,0:T(8,128)(2,1)}, u32[]{:S(2)}, u32[]{:S(2)}) %all-to-all-start.5) | async-done | bytes 2752544 | tf_op jit(solution)/shard_map/all_to_all | solution.py:227
  224.4 4.6 %all-to-all-start.6 = ((bf16[8,48,1792]{2,1,0:T(8,128)(2,1)}), bf16[8,48,1792]{2,1,0:T(8,128)(2,1)}, u32[]{:S(2)}, u32[]{:S(2)}) async-start(bf16[8,48,1792]{2,1,0:T(8,128)(2,1)} %bitcast.77), calls=%async_computation.6 | async-start | bytes 2752512 | tf_op jit(solution)/shard_map/all_to_all | solution.py:227
  229.0 6.9 %shard_map.134.own_ref = bf16[384,512]{1,0:T(8,128)(2,1)} custom-call(bf16[384,3584]{1,0:T(8,128)(2,1)} %bitcast.42.rows_ref, bf16[3584,512]{1,0:T(8,128)(2,1)} %bitcast.88, bf16[3584,512]{1,0:T(8,128)(2,1)} %bitcast.92), custom_call_target="tpu_custom_call" | custom-call | flops 2818572288 | bytes 10485760 | tf_op jit(solution)/shard_map/pallas_call | solution.py:78
  237.4 6.6 %collective-permute-done.14.mate_ref = bf16[384,512]{1,0:T(8,128)(2,1)S(1)} collective-permute-done((bf16[384,512]{1,0:T(8,128)(2,1)}, bf16[384,512]{1,0:T(8,128)(2,1)S(1)}, u32[]{:S(2)}, u32[]{:S(2)}) %collective-permute-start.14) | collective-permute-done | bytes 393248 | tf_op jit(solution)/shard_map/ppermute | solution.py:176
  245.0 2.7 shard_map.135
  248.8 5.9 %all-to-all-start.7 = ((bf16[8,48,1792]{2,1,0:T(8,128)(2,1)}), bf16[8,48,1792]{2,1,0:T(8,128)(2,1)S(1)}, u32[]{:S(2)}, u32[]{:S(2)}) async-start(bf16[8,48,1792]{2,1,0:T(8,128)(2,1)} %bitcast.74), calls=%async_computation.7 | async-start | bytes 2752512 | tf_op jit(solution)/shard_map/all_to_all | solution.py:227
  254.9 1.8 shard_map.136
  256.8 9.0 %collective-permute-start.15 = (bf16[64,1792]{1,0:T(8,128)(2,1)S(1)}, bf16[64,1792]{1,0:T(8,128)(2,1)S(1)}, u32[]{:S(2)}, u32[]{:S(2)}) collective-permute-start(bf16[64,1792]{1,0:T(8,128)(2,1)S(1)} %get-tuple-element.82), channel_id=1, source_target_pairs={{0,16},{1,17},{2,18},{3,19},{4,20},{5,21},{6,22},{7,23},{8,24},{9,... | collective-permute-start | bytes 688136 | tf_op jit(solution)/shard_map/ppermute | solution.py:187
  265.8 1.9 collective-permute-start.16
  268.8 3.7 %collective-permute-done.16 = bf16[64,1792]{1,0:T(8,128)(2,1)S(1)} collective-permute-done((bf16[64,1792]{1,0:T(8,128)(2,1)S(1)}, bf16[64,1792]{1,0:T(8,128)(2,1)S(1)}, u32[]{:S(2)}, u32[]{:S(2)}) %collective-permute-start.16) | collective-permute-done | bytes 229408 | tf_op jit(solution)/shard_map/ppermute | solution.py:187
  273.0 2.4 collective-permute-start.17
  275.4 3.0 %collective-permute-start.18 = (bf16[64,1792]{1,0:T(8,128)(2,1)S(1)}, bf16[64,1792]{1,0:T(8,128)(2,1)S(1)}, u32[]{:S(2)}, u32[]{:S(2)}) collective-permute-start(bf16[64,1792]{1,0:T(8,128)(2,1)S(1)} %get-tuple-element.79), channel_id=1, source_target_pairs={{0,241},{1,240},{2,243},{3,242},{4,245},{5,244},{6,247},{7,246},{8... | collective-permute-start | bytes 688136 | tf_op jit(solution)/shard_map/ppermute | solution.py:187
  279.2 6.1 %collective-permute-done.17 = bf16[64,1792]{1,0:T(8,128)(2,1)S(1)} collective-permute-done((bf16[64,1792]{1,0:T(8,128)(2,1)S(1)}, bf16[64,1792]{1,0:T(8,128)(2,1)S(1)}, u32[]{:S(2)}, u32[]{:S(2)}) %collective-permute-start.17) | collective-permute-done | bytes 229408 | tf_op jit(solution)/shard_map/ppermute | solution.py:187
  285.2 5.2 %collective-permute-done.18 = bf16[64,1792]{1,0:T(8,128)(2,1)S(1)} collective-permute-done((bf16[64,1792]{1,0:T(8,128)(2,1)S(1)}, bf16[64,1792]{1,0:T(8,128)(2,1)S(1)}, u32[]{:S(2)}, u32[]{:S(2)}) %collective-permute-start.18) | collective-permute-done | bytes 229408 | tf_op jit(solution)/shard_map/ppermute | solution.py:187
  (109 shorter events, 32.1 us)
Async XLA Ops:
  3.0 4.2 %collective-permute-start = (s32[4,64]{1,0:T(4,128)S(1)}, s32[4,64]{1,0:T(4,128)S(1)}, u32[]{:S(2)}, u32[]{:S(2)}) collective-permute-start(s32[4,64]{1,0:T(4,128)S(1)} %get-tuple-element.109), channel_id=1, source_target_pairs={{0,1},{1,0},{2,3},{3,2},{4,5},{5,4},{6,7},{7,6},{8,9},{9,8},{10,11... | collective-permute-start | bytes 3080 | tf_op jit(solution)/shard_map/ppermute | solution.py:176
  3.3 10.3 %collective-permute-start.1 = (bf16[64,3584]{1,0:T(8,128)(2,1)}, bf16[64,3584]{1,0:T(8,128)(2,1)S(1)}, u32[]{:S(2)}, u32[]{:S(2)}) collective-permute-start(bf16[64,3584]{1,0:T(8,128)(2,1)} %bitcast.79), channel_id=1, source_target_pairs={{16,17},{17,16},{18,19},{19,18},{20,21},{21,20},{22,23},{23,22},{2... | collective-permute-start | bytes 1376264 | tf_op jit(solution)/shard_map/ppermute | solution.py:179
  7.2 6.4 %collective-permute-start.2 = (bf16[64,3584]{1,0:T(8,128)(2,1)}, bf16[64,3584]{1,0:T(8,128)(2,1)S(1)}, u32[]{:S(2)}, u32[]{:S(2)}) collective-permute-start(bf16[64,3584]{1,0:T(8,128)(2,1)} %bitcast.80), channel_id=1, source_target_pairs={{0,1},{1,0},{2,3},{3,2},{4,5},{5,4},{6,7},{7,6},{8,9},{9,8},{10,11... | collective-permute-start | bytes 1376264 | tf_op jit(solution)/shard_map/ppermute | solution.py:179
  13.6 1.0 copy-start.18
  17.3 39.2 %all-to-all-start = ((bf16[8,48,3584]{2,1,0:T(8,128)(2,1)}), bf16[8,48,3584]{2,1,0:T(8,128)(2,1)}, u32[]{:S(2)}, u32[]{:S(2)}) async-start(bf16[8,48,3584]{2,1,0:T(8,128)(2,1)} %bitcast.26), calls=%async_computation | async-start | bytes 5505024 | tf_op jit(solution)/shard_map/all_to_all | solution.py:227
  23.7 2.4 copy-start.20
  23.7 3.0 %copy-start.19 = (bf16[1,64,3584]{2,1,0:T(8,128)(2,1)S(1)}, bf16[1,64,3584]{2,1,0:T(8,128)(2,1)}, u32[]{:S(2)}) copy-start(bf16[1,64,3584]{2,1,0:T(8,128)(2,1)} %param.11) | copy-start | bytes 1376260
  26.1 9.3 %copy-start.21 = (bf16[512,1792]{1,0:T(8,128)(2,1)}, bf16[512,1792]{1,0:T(8,128)(2,1)S(1)}, u32[]{:S(2)}) copy-start(bf16[512,1792]{1,0:T(8,128)(2,1)S(1)} %get-tuple-element.51) | copy-start | bytes 5505028
  26.1 7.8 %collective-permute-start.3 = (bf16[64,3584]{1,0:T(8,128)(2,1)S(1)}, bf16[64,3584]{1,0:T(8,128)(2,1)S(1)}, u32[]{:S(2)}, u32[]{:S(2)}) collective-permute-start(bf16[64,3584]{1,0:T(8,128)(2,1)S(1)} %bitcast.82), channel_id=1, source_target_pairs={{0,1},{1,0},{2,3},{3,2},{4,5},{5,4},{6,7},{7,6},{8,9},{9,8},{10,11... | collective-permute-start | bytes 1376264 | tf_op jit(solution)/shard_map/ppermute | solution.py:176
  26.7 8.7 %collective-permute-start.5 = (f32[4,64]{1,0:T(4,128)S(1)}, f32[4,64]{1,0:T(4,128)S(1)}, u32[]{:S(2)}, u32[]{:S(2)}) collective-permute-start(f32[4,64]{1,0:T(4,128)S(1)} %pad_maximum_fusion.2), channel_id=1, source_target_pairs={{0,1},{1,0},{2,3},{3,2},{4,5},{5,4},{6,7},{7,6},{8,9},{9,8},{10,11... | collective-permute-start | bytes 3080 | tf_op jit(solution)/shard_map/ppermute | solution.py:176
  34.0 22.6 %collective-permute-start.4 = (bf16[304,1792]{1,0:T(8,128)(2,1)S(1)}, bf16[304,1792]{1,0:T(8,128)(2,1)S(1)}, u32[]{:S(2)}, u32[]{:S(2)}) collective-permute-start(bf16[304,1792]{1,0:T(8,128)(2,1)S(1)} %slice.68), channel_id=1, source_target_pairs={{0,1},{1,0},{2,3},{3,2},{4,5},{5,4},{6,7},{7,6},{8,9},{9,8},{10,11... | collective-permute-start | bytes 3268616 | tf_op jit(solution)/shard_map/ppermute | solution.py:176
  36.5 1.6 copy-start.4
  56.6 32.1 %all-to-all-start.1 = ((bf16[8,48,3584]{2,1,0:T(8,128)(2,1)}), bf16[8,48,3584]{2,1,0:T(8,128)(2,1)}, u32[]{:S(2)}, u32[]{:S(2)}) async-start(bf16[8,48,3584]{2,1,0:T(8,128)(2,1)} %bitcast.71), calls=%async_computation.1 | async-start | bytes 5505024 | tf_op jit(solution)/shard_map/all_to_all | solution.py:227
  62.3 12.2 %collective-permute-start.7 = (bf16[208,1792]{1,0:T(8,128)(2,1)S(1)}, bf16[208,1792]{1,0:T(8,128)(2,1)S(1)}, u32[]{:S(2)}, u32[]{:S(2)}) collective-permute-start(bf16[208,1792]{1,0:T(8,128)(2,1)S(1)} %slice.75), channel_id=1, source_target_pairs={{0,1},{1,0},{2,3},{3,2},{4,5},{5,4},{6,7},{7,6},{8,9},{9,8},{10,11... | collective-permute-start | bytes 2236424 | tf_op jit(solution)/shard_map/ppermute | solution.py:176
  71.4 11.6 %collective-permute-start.6 = (bf16[384,512]{1,0:T(8,128)(2,1)}, bf16[384,512]{1,0:T(8,128)(2,1)S(1)}, u32[]{:S(2)}, u32[]{:S(2)}) collective-permute-start(bf16[384,512]{1,0:T(8,128)(2,1)} %shard_map.124.own_ref), channel_id=1, source_target_pairs={{0,1},{1,0},{2,3},{3,2},{4,5},{5,4},{6,7},{7,6},{8,9},{9,8},{10,11... | collective-permute-start | bytes 1179656 | tf_op jit(solution)/shard_map/ppermute | solution.py:176
  82.9 1.0 copy-start.14
  86.6 0.9 copy-start
  87.6 1.1 copy-start.10
  88.7 24.8 %all-to-all-start.2 = ((bf16[8,48,1792]{2,1,0:T(8,128)(2,1)}), bf16[8,48,1792]{2,1,0:T(8,128)(2,1)}, u32[]{:S(2)}, u32[]{:S(2)}) async-start(bf16[8,48,1792]{2,1,0:T(8,128)(2,1)} %bitcast.78), calls=%async_computation.2 | async-start | bytes 2752512 | tf_op jit(solution)/shard_map/all_to_all | solution.py:227
  94.3 14.3 %copy-start.1 = (bf16[208,1792]{1,0:T(8,128)(2,1)S(1)}, bf16[208,1792]{1,0:T(8,128)(2,1)}, u32[]{:S(2)}) copy-start(bf16[208,1792]{1,0:T(8,128)(2,1)} %copy-done) | copy-start | bytes 2236420
  101.2 7.4 %collective-permute-start.8 = (bf16[384,512]{1,0:T(8,128)(2,1)}, bf16[384,512]{1,0:T(8,128)(2,1)S(1)}, u32[]{:S(2)}, u32[]{:S(2)}) collective-permute-start(bf16[384,512]{1,0:T(8,128)(2,1)} %shard_map.126.own_ref), channel_id=1, source_target_pairs={{0,1},{1,0},{2,3},{3,2},{4,5},{5,4},{6,7},{7,6},{8,9},{9,8},{10,11... | collective-permute-start | bytes 1179656 | tf_op jit(solution)/shard_map/ppermute | solution.py:176
  108.6 1.0 copy-start.16
  112.3 1.2 copy-start.8
  113.5 35.9 %all-to-all-start.3 = ((bf16[8,48,1792]{2,1,0:T(8,128)(2,1)}), bf16[8,48,1792]{2,1,0:T(8,128)(2,1)}, u32[]{:S(2)}, u32[]{:S(2)}) async-start(bf16[8,48,1792]{2,1,0:T(8,128)(2,1)} %bitcast.76), calls=%async_computation.3 | async-start | bytes 2752512 | tf_op jit(solution)/shard_map/all_to_all | solution.py:227
  119.4 1.0 copy-start.11
  122.3 23.0 %collective-permute-start.10 = (bf16[128,1792]{1,0:T(8,128)(2,1)S(1)}, bf16[128,1792]{1,0:T(8,128)(2,1)S(1)}, u32[]{:S(2)}, u32[]{:S(2)}) collective-permute-start(bf16[128,1792]{1,0:T(8,128)(2,1)S(1)} %shard_map.128), channel_id=1, source_target_pairs={{0,17},{1,16},{2,19},{3,18},{4,21},{5,20},{6,23},{7,22},{8,25},{9,... | collective-permute-start | bytes 1376264 | tf_op jit(solution)/shard_map/ppermute | solution.py:187
  135.5 10.4 %collective-permute-start.9 = (bf16[128,1792]{1,0:T(8,128)(2,1)S(1)}, bf16[128,1792]{1,0:T(8,128)(2,1)S(1)}, u32[]{:S(2)}, u32[]{:S(2)}) collective-permute-start(bf16[128,1792]{1,0:T(8,128)(2,1)S(1)} %shard_map.128), channel_id=1, source_target_pairs={{0,16},{1,17},{2,18},{3,19},{4,20},{5,21},{6,22},{7,23},{8,24},{9,... | collective-permute-start | bytes 1376264 | tf_op jit(solution)/shard_map/ppermute | solution.py:187
  147.1 1.6 copy-start.5
  149.4 38.8 %all-to-all-start.4 = ((bf16[8,48,3584]{2,1,0:T(8,128)(2,1)}), bf16[8,48,3584]{2,1,0:T(8,128)(2,1)}, u32[]{:S(2)}, u32[]{:S(2)}) async-start(bf16[8,48,3584]{2,1,0:T(8,128)(2,1)} %bitcast.72), calls=%async_computation.4 | async-start | bytes 5505024 | tf_op jit(solution)/shard_map/all_to_all | solution.py:227
  157.5 10.7 %collective-permute-start.12 = (bf16[128,1792]{1,0:T(8,128)(2,1)S(1)}, bf16[128,1792]{1,0:T(8,128)(2,1)S(1)}, u32[]{:S(2)}, u32[]{:S(2)}) collective-permute-start(bf16[128,1792]{1,0:T(8,128)(2,1)S(1)} %shard_map.130), channel_id=1, source_target_pairs={{0,241},{1,240},{2,243},{3,242},{4,245},{5,244},{6,247},{7,246},{8... | collective-permute-start | bytes 1376264 | tf_op jit(solution)/shard_map/ppermute | solution.py:187
  157.8 14.0 %collective-permute-start.11 = (bf16[128,1792]{1,0:T(8,128)(2,1)S(1)}, bf16[128,1792]{1,0:T(8,128)(2,1)S(1)}, u32[]{:S(2)}, u32[]{:S(2)}) collective-permute-start(bf16[128,1792]{1,0:T(8,128)(2,1)S(1)} %shard_map.130), channel_id=1, source_target_pairs={{0,240},{1,241},{2,242},{3,243},{4,244},{5,245},{6,246},{7,247},{8... | collective-permute-start | bytes 1376264 | tf_op jit(solution)/shard_map/ppermute | solution.py:187
  173.1 1.6 copy-start.6
  188.2 36.2 %all-to-all-start.5 = ((bf16[8,48,3584]{2,1,0:T(8,128)(2,1)}), bf16[8,48,3584]{2,1,0:T(8,128)(2,1)}, u32[]{:S(2)}, u32[]{:S(2)}) async-start(bf16[8,48,3584]{2,1,0:T(8,128)(2,1)} %bitcast.73), calls=%async_computation.5 | async-start | bytes 5505024 | tf_op jit(solution)/shard_map/all_to_all | solution.py:227
  192.7 15.6 %copy-start.2 = (bf16[208,1792]{1,0:T(8,128)(2,1)S(1)}, bf16[208,1792]{1,0:T(8,128)(2,1)}, u32[]{:S(2)}) copy-start(bf16[208,1792]{1,0:T(8,128)(2,1)} %copy-done) | copy-start | bytes 2236420
  199.6 8.7 %collective-permute-start.13 = (bf16[384,512]{1,0:T(8,128)(2,1)}, bf16[384,512]{1,0:T(8,128)(2,1)S(1)}, u32[]{:S(2)}, u32[]{:S(2)}) collective-permute-start(bf16[384,512]{1,0:T(8,128)(2,1)} %shard_map.132.own_ref), channel_id=1, source_target_pairs={{0,1},{1,0},{2,3},{3,2},{4,5},{5,4},{6,7},{7,6},{8,9},{9,8},{10,11... | collective-permute-start | bytes 1179656 | tf_op jit(solution)/shard_map/ppermute | solution.py:176
  208.3 1.0 copy-start.17
  212.0 1.1 copy-start.9
  224.4 24.4 %all-to-all-start.6 = ((bf16[8,48,1792]{2,1,0:T(8,128)(2,1)}), bf16[8,48,1792]{2,1,0:T(8,128)(2,1)}, u32[]{:S(2)}, u32[]{:S(2)}) async-start(bf16[8,48,1792]{2,1,0:T(8,128)(2,1)} %bitcast.77), calls=%async_computation.6 | async-start | bytes 2752512 | tf_op jit(solution)/shard_map/all_to_all | solution.py:227
  229.0 15.0 %copy-start.3 = (bf16[208,1792]{1,0:T(8,128)(2,1)S(1)}, bf16[208,1792]{1,0:T(8,128)(2,1)}, u32[]{:S(2)}) copy-start(bf16[208,1792]{1,0:T(8,128)(2,1)} %copy-done) | copy-start | bytes 2236420
  235.8 8.1 %collective-permute-start.14 = (bf16[384,512]{1,0:T(8,128)(2,1)}, bf16[384,512]{1,0:T(8,128)(2,1)S(1)}, u32[]{:S(2)}, u32[]{:S(2)}) collective-permute-start(bf16[384,512]{1,0:T(8,128)(2,1)} %shard_map.134.own_ref), channel_id=1, source_target_pairs={{0,1},{1,0},{2,3},{3,2},{4,5},{5,4},{6,7},{7,6},{8,9},{9,8},{10,11... | collective-permute-start | bytes 1179656 | tf_op jit(solution)/shard_map/ppermute | solution.py:176
  244.0 1.0 copy-start.15
  247.7 1.1 copy-start.7
  248.8 6.1 %copy-start.13 = (bf16[128,1792]{1,0:T(8,128)(2,1)S(1)}, bf16[128,1792]{1,0:T(8,128)(2,1)}, u32[]{:S(2)}) copy-start(bf16[128,1792]{1,0:T(8,128)(2,1)} %copy-done.12) | copy-start | bytes 1376260
  248.8 23.7 %all-to-all-start.7 = ((bf16[8,48,1792]{2,1,0:T(8,128)(2,1)}), bf16[8,48,1792]{2,1,0:T(8,128)(2,1)S(1)}, u32[]{:S(2)}, u32[]{:S(2)}) async-start(bf16[8,48,1792]{2,1,0:T(8,128)(2,1)} %bitcast.74), calls=%async_computation.7 | async-start | bytes 2752512 | tf_op jit(solution)/shard_map/all_to_all | solution.py:227
  256.8 12.0 %collective-permute-start.15 = (bf16[64,1792]{1,0:T(8,128)(2,1)S(1)}, bf16[64,1792]{1,0:T(8,128)(2,1)S(1)}, u32[]{:S(2)}, u32[]{:S(2)}) collective-permute-start(bf16[64,1792]{1,0:T(8,128)(2,1)S(1)} %get-tuple-element.82), channel_id=1, source_target_pairs={{0,16},{1,17},{2,18},{3,19},{4,20},{5,21},{6,22},{7,23},{8,24},{9,... | collective-permute-start | bytes 688136 | tf_op jit(solution)/shard_map/ppermute | solution.py:187
  265.8 6.6 %collective-permute-start.16 = (bf16[64,1792]{1,0:T(8,128)(2,1)S(1)}, bf16[64,1792]{1,0:T(8,128)(2,1)S(1)}, u32[]{:S(2)}, u32[]{:S(2)}) collective-permute-start(bf16[64,1792]{1,0:T(8,128)(2,1)S(1)} %get-tuple-element.83), channel_id=1, source_target_pairs={{0,17},{1,16},{2,19},{3,18},{4,21},{5,20},{6,23},{7,22},{8,25},{9,... | collective-permute-start | bytes 688136 | tf_op jit(solution)/shard_map/ppermute | solution.py:187
  273.0 12.2 %collective-permute-start.17 = (bf16[64,1792]{1,0:T(8,128)(2,1)S(1)}, bf16[64,1792]{1,0:T(8,128)(2,1)S(1)}, u32[]{:S(2)}, u32[]{:S(2)}) collective-permute-start(bf16[64,1792]{1,0:T(8,128)(2,1)S(1)} %get-tuple-element.78), channel_id=1, source_target_pairs={{0,240},{1,241},{2,242},{3,243},{4,244},{5,245},{6,246},{7,247},{8... | collective-permute-start | bytes 688136 | tf_op jit(solution)/shard_map/ppermute | solution.py:187
  275.4 15.0 %collective-permute-start.18 = (bf16[64,1792]{1,0:T(8,128)(2,1)S(1)}, bf16[64,1792]{1,0:T(8,128)(2,1)S(1)}, u32[]{:S(2)}, u32[]{:S(2)}) collective-permute-start(bf16[64,1792]{1,0:T(8,128)(2,1)S(1)} %get-tuple-element.79), channel_id=1, source_target_pairs={{0,241},{1,240},{2,243},{3,242},{4,245},{5,244},{6,247},{7,246},{8... | collective-permute-start | bytes 688136 | tf_op jit(solution)/shard_map/ppermute | solution.py:187
  (1 other events, 0.8 us)

commit v4 on v3

--- a/solution.py
+++ b/solution.py
@@ -110,7 +110,7 @@
 def down(own, mate, own_rows, mate_rows):
     count, depth = own.shape
     width = own_rows.shape[1]
-    block = width // 2
+    block = width
     whole = pl.BlockSpec((count, depth), lambda j: (0, 0))
     return pl.pallas_call(
         down_kernel,

time: 292 us -> 290 us (level)
  Pallas kernels: 50.2 us -> 47.1 us
    pallas_call x4, Pallas kernels: 10.8 us -> 7.71 us  [down(): pl.pallas_call(down_kernel, grid=(width // block,), in_specs=[whole, whol...]
  transfers between devices with their start and end apart: 27 -> 27, of which waited for: 18 -> 18; matrix products, arithmetic and copies ran while one was open for 2% -> 2% of each run, Pallas kernels for 16% -> 15%
where the time goes in v4:
time: 290 us; the launch traced here: 289 us
  waiting for transfers between devices  127 us (44%)
  starting transfers between devices  86.3 us (30%)
  Pallas kernels  47.1 us (16%)
  local copies, waits for them, and re-layouts  23 us (8%)
  other arithmetic  4.32 us (1%)
    ppermute x9, waiting for transfers between devices, to_mate(): return lax.ppermute(array, 'expert', mates)  56.7 us
    all_to_all x8, starting transfers between devices, across(): lax.all_to_all(array, 'expert', 0, 0, axis_index_groups=sides, tiled=True)  43.2 us
    ppermute x8, waiting for transfers between devices, to_section(): lax.ppermute(array, ('section', 'expert'), [(s * lanes + i, (s + by) % se...  39.2 us
    ppermute x8, starting transfers between devices, to_section(): lax.ppermute(array, ('section', 'expert'), [(s * lanes + i, (s + by) % se...  30.9 us
    pallas_call x4, Pallas kernels, hidden(): pl.pallas_call(hidden_kernel, grid=(width // block,), in_specs=[pl.BlockS...  27.4 us
    all_to_all x8, waiting for transfers between devices, across(): lax.all_to_all(array, 'expert', 0, 0, axis_index_groups=sides, tiled=True)  25.7 us
    unnamed x44, local copies, waits for them, and re-layouts  16.9 us
    ppermute x9, starting transfers between devices, to_mate(): return lax.ppermute(array, 'expert', mates)  8.33 us
  transfers between devices with their start and end apart: 27, of which 18 were waited for; matrix products, arithmetic and copies ran while one was open for 2% of the time, Pallas kernels for 15%

profile of v4, /device:TPU:73, one launch (start us, length us, event | category | flops | bytes accessed | tf_op | source)
XLA Modules:
  0.0 289.0 jit_solution(4232476179266124780)
XLA Ops:
  3.3 3.2 %collective-permute-start.1 = (bf16[64,3584]{1,0:T(8,128)(2,1)}, bf16[64,3584]{1,0:T(8,128)(2,1)S(1)}, u32[]{:S(2)}, u32[]{:S(2)}) collective-permute-start(bf16[64,3584]{1,0:T(8,128)(2,1)} %bitcast.79), channel_id=1, source_target_pairs={{16,17},{17,16},{18,19},{19,18},{20,21},{21,20},{22,23},{23,22},{2... | collective-permute-start | bytes 1376264 | tf_op jit(solution)/shard_map/ppermute | solution.py:179
  8.0 5.6 %collective-permute-done.1.refs_0_ = bf16[64,3584]{1,0:T(8,128)(2,1)S(1)} collective-permute-done((bf16[64,3584]{1,0:T(8,128)(2,1)}, bf16[64,3584]{1,0:T(8,128)(2,1)S(1)}, u32[]{:S(2)}, u32[]{:S(2)}) %collective-permute-start.1) | collective-permute-done | bytes 458784 | tf_op jit(solution)/shard_map/ppermute | solution.py:179
  14.6 2.7 shard_map.122
  17.3 6.4 %all-to-all-start = ((bf16[8,48,3584]{2,1,0:T(8,128)(2,1)}), bf16[8,48,3584]{2,1,0:T(8,128)(2,1)}, u32[]{:S(2)}, u32[]{:S(2)}) async-start(bf16[8,48,3584]{2,1,0:T(8,128)(2,1)} %bitcast.26), calls=%async_computation | async-start | bytes 5505024 | tf_op jit(solution)/shard_map/all_to_all | solution.py:227
  23.7 2.4 dynamic-slice_bitcast_fusion
  27.8 6.1 %collective-permute-done.3.refs_0_ = bf16[64,3584]{1,0:T(8,128)(2,1)S(1)} collective-permute-done((bf16[64,3584]{1,0:T(8,128)(2,1)S(1)}, bf16[64,3584]{1,0:T(8,128)(2,1)S(1)}, u32[]{:S(2)}, u32[]{:S(2)}) %collective-permute-start.3) | collective-permute-done | bytes 458784 | tf_op jit(solution)/shard_map/ppermute | solution.py:176
  36.5 1.6 copy-done.4
  38.2 18.4 %collective-permute-done.4.refs_0_ = bf16[304,1792]{1,0:T(8,128)(2,1)S(1)} collective-permute-done((bf16[304,1792]{1,0:T(8,128)(2,1)S(1)}, bf16[304,1792]{1,0:T(8,128)(2,1)S(1)}, u32[]{:S(2)}, u32[]{:S(2)}) %collective-permute-start.4) | collective-permute-done | bytes 1089568 | tf_op jit(solution)/shard_map/ppermute | solution.py:176
  56.6 4.5 %all-to-all-start.1 = ((bf16[8,48,3584]{2,1,0:T(8,128)(2,1)}), bf16[8,48,3584]{2,1,0:T(8,128)(2,1)}, u32[]{:S(2)}, u32[]{:S(2)}) async-start(bf16[8,48,3584]{2,1,0:T(8,128)(2,1)} %bitcast.71), calls=%async_computation.1 | async-start | bytes 5505024 | tf_op jit(solution)/shard_map/all_to_all | solution.py:227
  62.3 2.3 collective-permute-start.7
  64.6 6.8 %shard_map.124.own_ref = bf16[384,512]{1,0:T(8,128)(2,1)} custom-call(bf16[384,3584]{1,0:T(8,128)(2,1)} %bitcast.27.rows_ref, bf16[3584,512]{1,0:T(8,128)(2,1)} %bitcast.85, bf16[3584,512]{1,0:T(8,128)(2,1)} %bitcast.89), custom_call_target="tpu_custom_call" | custom-call | flops 2818572288 | bytes 10485760 | tf_op jit(solution)/shard_map/pallas_call | solution.py:78
  71.4 3.1 %collective-permute-done.7.refs_1_ = bf16[208,1792]{1,0:T(8,128)(2,1)S(1)} collective-permute-done((bf16[208,1792]{1,0:T(8,128)(2,1)S(1)}, bf16[208,1792]{1,0:T(8,128)(2,1)S(1)}, u32[]{:S(2)}, u32[]{:S(2)}) %collective-permute-start.7) | collective-permute-done | bytes 745504 | tf_op jit(solution)/shard_map/ppermute | solution.py:176
  74.5 8.4 %collective-permute-done.6.mate_ref = bf16[384,512]{1,0:T(8,128)(2,1)S(1)} collective-permute-done((bf16[384,512]{1,0:T(8,128)(2,1)}, bf16[384,512]{1,0:T(8,128)(2,1)S(1)}, u32[]{:S(2)}, u32[]{:S(2)}) %collective-permute-start.6) | collective-permute-done | bytes 393248 | tf_op jit(solution)/shard_map/ppermute | solution.py:176
  83.9 1.9 shard_map.125
  87.9 5.6 %all-to-all-start.2 = ((bf16[8,48,1792]{2,1,0:T(8,128)(2,1)}), bf16[8,48,1792]{2,1,0:T(8,128)(2,1)}, u32[]{:S(2)}, u32[]{:S(2)}) async-start(bf16[8,48,1792]{2,1,0:T(8,128)(2,1)} %bitcast.78), calls=%async_computation.2 | async-start | bytes 2752512 | tf_op jit(solution)/shard_map/all_to_all | solution.py:227
  93.5 6.9 %shard_map.126.own_ref = bf16[384,512]{1,0:T(8,128)(2,1)} custom-call(bf16[384,3584]{1,0:T(8,128)(2,1)} %bitcast.32.rows_ref, bf16[3584,512]{1,0:T(8,128)(2,1)} %bitcast.86, bf16[3584,512]{1,0:T(8,128)(2,1)} %bitcast.90), custom_call_target="tpu_custom_call" | custom-call | flops 2818572288 | bytes 10485760 | tf_op jit(solution)/shard_map/pallas_call | solution.py:78
  100.4 1.6 collective-permute-start.8
  102.0 5.8 %collective-permute-done.8.mate_ref = bf16[384,512]{1,0:T(8,128)(2,1)S(1)} collective-permute-done((bf16[384,512]{1,0:T(8,128)(2,1)}, bf16[384,512]{1,0:T(8,128)(2,1)S(1)}, u32[]{:S(2)}, u32[]{:S(2)}) %collective-permute-start.8) | collective-permute-done | bytes 393248 | tf_op jit(solution)/shard_map/ppermute | solution.py:176
  108.8 1.9 shard_map.127
  111.9 5.7 %all-to-all-start.3 = ((bf16[8,48,1792]{2,1,0:T(8,128)(2,1)}), bf16[8,48,1792]{2,1,0:T(8,128)(2,1)}, u32[]{:S(2)}, u32[]{:S(2)}) async-start(bf16[8,48,1792]{2,1,0:T(8,128)(2,1)} %bitcast.76), calls=%async_computation.3 | async-start | bytes 2752512 | tf_op jit(solution)/shard_map/all_to_all | solution.py:227
  118.9 1.8 shard_map.128
  120.7 13.3 %collective-permute-start.10 = (bf16[128,1792]{1,0:T(8,128)(2,1)S(1)}, bf16[128,1792]{1,0:T(8,128)(2,1)S(1)}, u32[]{:S(2)}, u32[]{:S(2)}) collective-permute-start(bf16[128,1792]{1,0:T(8,128)(2,1)S(1)} %shard_map.128), channel_id=1, source_target_pairs={{0,17},{1,16},{2,19},{3,18},{4,21},{5,20},{6,23},{7,22},{8,25},{9,... | collective-permute-start | bytes 1376264 | tf_op jit(solution)/shard_map/ppermute | solution.py:187
  134.0 9.7 %collective-permute-done.10.far_ref = bf16[128,1792]{1,0:T(8,128)(2,1)S(1)} collective-permute-done((bf16[128,1792]{1,0:T(8,128)(2,1)S(1)}, bf16[128,1792]{1,0:T(8,128)(2,1)S(1)}, u32[]{:S(2)}, u32[]{:S(2)}) %collective-permute-start.10) | collective-permute-done | bytes 458784 | tf_op jit(solution)/shard_map/ppermute | solution.py:187
  145.6 1.5 copy-done.5
  147.9 6.0 %all-to-all-start.4 = ((bf16[8,48,3584]{2,1,0:T(8,128)(2,1)}), bf16[8,48,3584]{2,1,0:T(8,128)(2,1)}, u32[]{:S(2)}, u32[]{:S(2)}) async-start(bf16[8,48,3584]{2,1,0:T(8,128)(2,1)} %bitcast.72), calls=%async_computation.4 | async-start | bytes 5505024 | tf_op jit(solution)/shard_map/all_to_all | solution.py:227
  154.2 1.8 shard_map.130
  157.3 9.3 %collective-permute-done.12.far_ref = bf16[128,1792]{1,0:T(8,128)(2,1)S(1)} collective-permute-done((bf16[128,1792]{1,0:T(8,128)(2,1)S(1)}, bf16[128,1792]{1,0:T(8,128)(2,1)S(1)}, u32[]{:S(2)}, u32[]{:S(2)}) %collective-permute-start.12) | collective-permute-done | bytes 458784 | tf_op jit(solution)/shard_map/ppermute | solution.py:187
  166.6 3.7 %collective-permute-done.11.near_ref.state_ref = bf16[128,1792]{1,0:T(8,128)(2,1)S(1)} collective-permute-done((bf16[128,1792]{1,0:T(8,128)(2,1)S(1)}, bf16[128,1792]{1,0:T(8,128)(2,1)S(1)}, u32[]{:S(2)}, u32[]{:S(2)}) %collective-permute-start.11) | collective-permute-done | bytes 458784 | tf_op jit(solution)/shard_map/ppermute | solution.py:187
  171.6 1.6 copy-done.6
  173.2 13.6 %all-to-all-done.4 = bf16[8,48,3584]{2,1,0:T(8,128)(2,1)} async-done(((bf16[8,48,3584]{2,1,0:T(8,128)(2,1)}), bf16[8,48,3584]{2,1,0:T(8,128)(2,1)}, u32[]{:S(2)}, u32[]{:S(2)}) %all-to-all-start.4) | async-done | bytes 2752544 | tf_op jit(solution)/shard_map/all_to_all | solution.py:227
  186.7 4.4 %all-to-all-start.5 = ((bf16[8,48,3584]{2,1,0:T(8,128)(2,1)}), bf16[8,48,3584]{2,1,0:T(8,128)(2,1)}, u32[]{:S(2)}, u32[]{:S(2)}) async-start(bf16[8,48,3584]{2,1,0:T(8,128)(2,1)} %bitcast.73), calls=%async_computation.5 | async-start | bytes 5505024 | tf_op jit(solution)/shard_map/all_to_all | solution.py:227
  191.2 6.9 %shard_map.132.own_ref = bf16[384,512]{1,0:T(8,128)(2,1)} custom-call(bf16[384,3584]{1,0:T(8,128)(2,1)} %bitcast.40.rows_ref, bf16[3584,512]{1,0:T(8,128)(2,1)} %bitcast.87, bf16[3584,512]{1,0:T(8,128)(2,1)} %bitcast.91), custom_call_target="tpu_custom_call" | custom-call | flops 2818572288 | bytes 10485760 | tf_op jit(solution)/shard_map/pallas_call | solution.py:78
  198.4 8.4 %collective-permute-done.13.mate_ref = bf16[384,512]{1,0:T(8,128)(2,1)S(1)} collective-permute-done((bf16[384,512]{1,0:T(8,128)(2,1)}, bf16[384,512]{1,0:T(8,128)(2,1)S(1)}, u32[]{:S(2)}, u32[]{:S(2)}) %collective-permute-start.13) | collective-permute-done | bytes 393248 | tf_op jit(solution)/shard_map/ppermute | solution.py:176
  207.8 1.9 shard_map.133
  210.8 12.1 %all-to-all-done.5 = bf16[8,48,3584]{2,1,0:T(8,128)(2,1)} async-done(((bf16[8,48,3584]{2,1,0:T(8,128)(2,1)}), bf16[8,48,3584]{2,1,0:T(8,128)(2,1)}, u32[]{:S(2)}, u32[]{:S(2)}) %all-to-all-start.5) | async-done | bytes 2752544 | tf_op jit(solution)/shard_map/all_to_all | solution.py:227
  222.9 4.6 %all-to-all-start.6 = ((bf16[8,48,1792]{2,1,0:T(8,128)(2,1)}), bf16[8,48,1792]{2,1,0:T(8,128)(2,1)}, u32[]{:S(2)}, u32[]{:S(2)}) async-start(bf16[8,48,1792]{2,1,0:T(8,128)(2,1)} %bitcast.77), calls=%async_computation.6 | async-start | bytes 2752512 | tf_op jit(solution)/shard_map/all_to_all | solution.py:227
  227.5 6.9 %shard_map.134.own_ref = bf16[384,512]{1,0:T(8,128)(2,1)} custom-call(bf16[384,3584]{1,0:T(8,128)(2,1)} %bitcast.42.rows_ref, bf16[3584,512]{1,0:T(8,128)(2,1)} %bitcast.88, bf16[3584,512]{1,0:T(8,128)(2,1)} %bitcast.92), custom_call_target="tpu_custom_call" | custom-call | flops 2818572288 | bytes 10485760 | tf_op jit(solution)/shard_map/pallas_call | solution.py:78
  235.9 6.6 %collective-permute-done.14.mate_ref = bf16[384,512]{1,0:T(8,128)(2,1)S(1)} collective-permute-done((bf16[384,512]{1,0:T(8,128)(2,1)}, bf16[384,512]{1,0:T(8,128)(2,1)S(1)}, u32[]{:S(2)}, u32[]{:S(2)}) %collective-permute-start.14) | collective-permute-done | bytes 393248 | tf_op jit(solution)/shard_map/ppermute | solution.py:176
  243.5 1.9 shard_map.135
  246.5 5.9 %all-to-all-start.7 = ((bf16[8,48,1792]{2,1,0:T(8,128)(2,1)}), bf16[8,48,1792]{2,1,0:T(8,128)(2,1)S(1)}, u32[]{:S(2)}, u32[]{:S(2)}) async-start(bf16[8,48,1792]{2,1,0:T(8,128)(2,1)} %bitcast.74), calls=%async_computation.7 | async-start | bytes 2752512 | tf_op jit(solution)/shard_map/all_to_all | solution.py:227
  252.7 1.8 shard_map.136
  254.5 9.1 %collective-permute-start.15 = (bf16[64,1792]{1,0:T(8,128)(2,1)S(1)}, bf16[64,1792]{1,0:T(8,128)(2,1)S(1)}, u32[]{:S(2)}, u32[]{:S(2)}) collective-permute-start(bf16[64,1792]{1,0:T(8,128)(2,1)S(1)} %get-tuple-element.82), channel_id=1, source_target_pairs={{0,16},{1,17},{2,18},{3,19},{4,20},{5,21},{6,22},{7,23},{8,24},{9,... | collective-permute-start | bytes 688136 | tf_op jit(solution)/shard_map/ppermute | solution.py:187
  263.6 1.9 collective-permute-start.16
  266.5 3.7 %collective-permute-done.16 = bf16[64,1792]{1,0:T(8,128)(2,1)S(1)} collective-permute-done((bf16[64,1792]{1,0:T(8,128)(2,1)S(1)}, bf16[64,1792]{1,0:T(8,128)(2,1)S(1)}, u32[]{:S(2)}, u32[]{:S(2)}) %collective-permute-start.16) | collective-permute-done | bytes 229408 | tf_op jit(solution)/shard_map/ppermute | solution.py:187
  270.8 2.4 collective-permute-start.17
  273.1 3.0 %collective-permute-start.18 = (bf16[64,1792]{1,0:T(8,128)(2,1)S(1)}, bf16[64,1792]{1,0:T(8,128)(2,1)S(1)}, u32[]{:S(2)}, u32[]{:S(2)}) collective-permute-start(bf16[64,1792]{1,0:T(8,128)(2,1)S(1)} %get-tuple-element.79), channel_id=1, source_target_pairs={{0,241},{1,240},{2,243},{3,242},{4,245},{5,244},{6,247},{7,246},{8... | collective-permute-start | bytes 688136 | tf_op jit(solution)/shard_map/ppermute | solution.py:187
  276.9 6.1 %collective-permute-done.17 = bf16[64,1792]{1,0:T(8,128)(2,1)S(1)} collective-permute-done((bf16[64,1792]{1,0:T(8,128)(2,1)S(1)}, bf16[64,1792]{1,0:T(8,128)(2,1)S(1)}, u32[]{:S(2)}, u32[]{:S(2)}) %collective-permute-start.17) | collective-permute-done | bytes 229408 | tf_op jit(solution)/shard_map/ppermute | solution.py:187
  283.0 5.2 %collective-permute-done.18 = bf16[64,1792]{1,0:T(8,128)(2,1)S(1)} collective-permute-done((bf16[64,1792]{1,0:T(8,128)(2,1)S(1)}, bf16[64,1792]{1,0:T(8,128)(2,1)S(1)}, u32[]{:S(2)}, u32[]{:S(2)}) %collective-permute-start.18) | collective-permute-done | bytes 229408 | tf_op jit(solution)/shard_map/ppermute | solution.py:187
  (109 shorter events, 32.1 us)
Async XLA Ops:
  3.0 4.2 %collective-permute-start = (s32[4,64]{1,0:T(4,128)S(1)}, s32[4,64]{1,0:T(4,128)S(1)}, u32[]{:S(2)}, u32[]{:S(2)}) collective-permute-start(s32[4,64]{1,0:T(4,128)S(1)} %get-tuple-element.109), channel_id=1, source_target_pairs={{0,1},{1,0},{2,3},{3,2},{4,5},{5,4},{6,7},{7,6},{8,9},{9,8},{10,11... | collective-permute-start | bytes 3080 | tf_op jit(solution)/shard_map/ppermute | solution.py:176
  3.3 10.3 %collective-permute-start.1 = (bf16[64,3584]{1,0:T(8,128)(2,1)}, bf16[64,3584]{1,0:T(8,128)(2,1)S(1)}, u32[]{:S(2)}, u32[]{:S(2)}) collective-permute-start(bf16[64,3584]{1,0:T(8,128)(2,1)} %bitcast.79), channel_id=1, source_target_pairs={{16,17},{17,16},{18,19},{19,18},{20,21},{21,20},{22,23},{23,22},{2... | collective-permute-start | bytes 1376264 | tf_op jit(solution)/shard_map/ppermute | solution.py:179
  7.2 6.4 %collective-permute-start.2 = (bf16[64,3584]{1,0:T(8,128)(2,1)}, bf16[64,3584]{1,0:T(8,128)(2,1)S(1)}, u32[]{:S(2)}, u32[]{:S(2)}) collective-permute-start(bf16[64,3584]{1,0:T(8,128)(2,1)} %bitcast.80), channel_id=1, source_target_pairs={{0,1},{1,0},{2,3},{3,2},{4,5},{5,4},{6,7},{7,6},{8,9},{9,8},{10,11... | collective-permute-start | bytes 1376264 | tf_op jit(solution)/shard_map/ppermute | solution.py:179
  13.6 1.0 copy-start.18
  17.3 39.2 %all-to-all-start = ((bf16[8,48,3584]{2,1,0:T(8,128)(2,1)}), bf16[8,48,3584]{2,1,0:T(8,128)(2,1)}, u32[]{:S(2)}, u32[]{:S(2)}) async-start(bf16[8,48,3584]{2,1,0:T(8,128)(2,1)} %bitcast.26), calls=%async_computation | async-start | bytes 5505024 | tf_op jit(solution)/shard_map/all_to_all | solution.py:227
  23.7 2.4 copy-start.20
  23.7 3.0 %copy-start.19 = (bf16[1,64,3584]{2,1,0:T(8,128)(2,1)S(1)}, bf16[1,64,3584]{2,1,0:T(8,128)(2,1)}, u32[]{:S(2)}) copy-start(bf16[1,64,3584]{2,1,0:T(8,128)(2,1)} %param.11) | copy-start | bytes 1376260
  26.1 9.3 %copy-start.21 = (bf16[512,1792]{1,0:T(8,128)(2,1)}, bf16[512,1792]{1,0:T(8,128)(2,1)S(1)}, u32[]{:S(2)}) copy-start(bf16[512,1792]{1,0:T(8,128)(2,1)S(1)} %get-tuple-element.51) | copy-start | bytes 5505028
  26.1 7.8 %collective-permute-start.3 = (bf16[64,3584]{1,0:T(8,128)(2,1)S(1)}, bf16[64,3584]{1,0:T(8,128)(2,1)S(1)}, u32[]{:S(2)}, u32[]{:S(2)}) collective-permute-start(bf16[64,3584]{1,0:T(8,128)(2,1)S(1)} %bitcast.82), channel_id=1, source_target_pairs={{0,1},{1,0},{2,3},{3,2},{4,5},{5,4},{6,7},{7,6},{8,9},{9,8},{10,11... | collective-permute-start | bytes 1376264 | tf_op jit(solution)/shard_map/ppermute | solution.py:176
  26.7 8.7 %collective-permute-start.5 = (f32[4,64]{1,0:T(4,128)S(1)}, f32[4,64]{1,0:T(4,128)S(1)}, u32[]{:S(2)}, u32[]{:S(2)}) collective-permute-start(f32[4,64]{1,0:T(4,128)S(1)} %pad_maximum_fusion.2), channel_id=1, source_target_pairs={{0,1},{1,0},{2,3},{3,2},{4,5},{5,4},{6,7},{7,6},{8,9},{9,8},{10,11... | collective-permute-start | bytes 3080 | tf_op jit(solution)/shard_map/ppermute | solution.py:176
  34.0 22.6 %collective-permute-start.4 = (bf16[304,1792]{1,0:T(8,128)(2,1)S(1)}, bf16[304,1792]{1,0:T(8,128)(2,1)S(1)}, u32[]{:S(2)}, u32[]{:S(2)}) collective-permute-start(bf16[304,1792]{1,0:T(8,128)(2,1)S(1)} %slice.68), channel_id=1, source_target_pairs={{0,1},{1,0},{2,3},{3,2},{4,5},{5,4},{6,7},{7,6},{8,9},{9,8},{10,11... | collective-permute-start | bytes 3268616 | tf_op jit(solution)/shard_map/ppermute | solution.py:176
  36.5 1.6 copy-start.4
  56.6 31.3 %all-to-all-start.1 = ((bf16[8,48,3584]{2,1,0:T(8,128)(2,1)}), bf16[8,48,3584]{2,1,0:T(8,128)(2,1)}, u32[]{:S(2)}, u32[]{:S(2)}) async-start(bf16[8,48,3584]{2,1,0:T(8,128)(2,1)} %bitcast.71), calls=%async_computation.1 | async-start | bytes 5505024 | tf_op jit(solution)/shard_map/all_to_all | solution.py:227
  62.3 12.2 %collective-permute-start.7 = (bf16[208,1792]{1,0:T(8,128)(2,1)S(1)}, bf16[208,1792]{1,0:T(8,128)(2,1)S(1)}, u32[]{:S(2)}, u32[]{:S(2)}) collective-permute-start(bf16[208,1792]{1,0:T(8,128)(2,1)S(1)} %slice.75), channel_id=1, source_target_pairs={{0,1},{1,0},{2,3},{3,2},{4,5},{5,4},{6,7},{7,6},{8,9},{9,8},{10,11... | collective-permute-start | bytes 2236424 | tf_op jit(solution)/shard_map/ppermute | solution.py:176
  71.4 11.6 %collective-permute-start.6 = (bf16[384,512]{1,0:T(8,128)(2,1)}, bf16[384,512]{1,0:T(8,128)(2,1)S(1)}, u32[]{:S(2)}, u32[]{:S(2)}) collective-permute-start(bf16[384,512]{1,0:T(8,128)(2,1)} %shard_map.124.own_ref), channel_id=1, source_target_pairs={{0,1},{1,0},{2,3},{3,2},{4,5},{5,4},{6,7},{7,6},{8,9},{9,8},{10,11... | collective-permute-start | bytes 1179656 | tf_op jit(solution)/shard_map/ppermute | solution.py:176
  82.9 1.0 copy-start.14
  85.9 0.9 copy-start
  86.8 1.1 copy-start.10
  87.9 24.0 %all-to-all-start.2 = ((bf16[8,48,1792]{2,1,0:T(8,128)(2,1)}), bf16[8,48,1792]{2,1,0:T(8,128)(2,1)}, u32[]{:S(2)}, u32[]{:S(2)}) async-start(bf16[8,48,1792]{2,1,0:T(8,128)(2,1)} %bitcast.78), calls=%async_computation.2 | async-start | bytes 2752512 | tf_op jit(solution)/shard_map/all_to_all | solution.py:227
  93.5 14.3 %copy-start.1 = (bf16[208,1792]{1,0:T(8,128)(2,1)S(1)}, bf16[208,1792]{1,0:T(8,128)(2,1)}, u32[]{:S(2)}) copy-start(bf16[208,1792]{1,0:T(8,128)(2,1)} %copy-done) | copy-start | bytes 2236420
  100.4 7.4 %collective-permute-start.8 = (bf16[384,512]{1,0:T(8,128)(2,1)}, bf16[384,512]{1,0:T(8,128)(2,1)S(1)}, u32[]{:S(2)}, u32[]{:S(2)}) collective-permute-start(bf16[384,512]{1,0:T(8,128)(2,1)} %shard_map.126.own_ref), channel_id=1, source_target_pairs={{0,1},{1,0},{2,3},{3,2},{4,5},{5,4},{6,7},{7,6},{8,9},{9,8},{10,11... | collective-permute-start | bytes 1179656 | tf_op jit(solution)/shard_map/ppermute | solution.py:176
  107.8 1.0 copy-start.16
  110.7 1.2 copy-start.8
  111.9 36.0 %all-to-all-start.3 = ((bf16[8,48,1792]{2,1,0:T(8,128)(2,1)}), bf16[8,48,1792]{2,1,0:T(8,128)(2,1)}, u32[]{:S(2)}, u32[]{:S(2)}) async-start(bf16[8,48,1792]{2,1,0:T(8,128)(2,1)} %bitcast.76), calls=%async_computation.3 | async-start | bytes 2752512 | tf_op jit(solution)/shard_map/all_to_all | solution.py:227
  117.9 1.0 copy-start.11
  120.7 23.0 %collective-permute-start.10 = (bf16[128,1792]{1,0:T(8,128)(2,1)S(1)}, bf16[128,1792]{1,0:T(8,128)(2,1)S(1)}, u32[]{:S(2)}, u32[]{:S(2)}) collective-permute-start(bf16[128,1792]{1,0:T(8,128)(2,1)S(1)} %shard_map.128), channel_id=1, source_target_pairs={{0,17},{1,16},{2,19},{3,18},{4,21},{5,20},{6,23},{7,22},{8,25},{9,... | collective-permute-start | bytes 1376264 | tf_op jit(solution)/shard_map/ppermute | solution.py:187
  134.0 10.4 %collective-permute-start.9 = (bf16[128,1792]{1,0:T(8,128)(2,1)S(1)}, bf16[128,1792]{1,0:T(8,128)(2,1)S(1)}, u32[]{:S(2)}, u32[]{:S(2)}) collective-permute-start(bf16[128,1792]{1,0:T(8,128)(2,1)S(1)} %shard_map.128), channel_id=1, source_target_pairs={{0,16},{1,17},{2,18},{3,19},{4,20},{5,21},{6,22},{7,23},{8,24},{9,... | collective-permute-start | bytes 1376264 | tf_op jit(solution)/shard_map/ppermute | solution.py:187
  145.6 1.6 copy-start.5
  147.9 38.8 %all-to-all-start.4 = ((bf16[8,48,3584]{2,1,0:T(8,128)(2,1)}), bf16[8,48,3584]{2,1,0:T(8,128)(2,1)}, u32[]{:S(2)}, u32[]{:S(2)}) async-start(bf16[8,48,3584]{2,1,0:T(8,128)(2,1)} %bitcast.72), calls=%async_computation.4 | async-start | bytes 5505024 | tf_op jit(solution)/shard_map/all_to_all | solution.py:227
  156.0 10.7 %collective-permute-start.12 = (bf16[128,1792]{1,0:T(8,128)(2,1)S(1)}, bf16[128,1792]{1,0:T(8,128)(2,1)S(1)}, u32[]{:S(2)}, u32[]{:S(2)}) collective-permute-start(bf16[128,1792]{1,0:T(8,128)(2,1)S(1)} %shard_map.130), channel_id=1, source_target_pairs={{0,241},{1,240},{2,243},{3,242},{4,245},{5,244},{6,247},{7,246},{8... | collective-permute-start | bytes 1376264 | tf_op jit(solution)/shard_map/ppermute | solution.py:187
  156.3 14.0 %collective-permute-start.11 = (bf16[128,1792]{1,0:T(8,128)(2,1)S(1)}, bf16[128,1792]{1,0:T(8,128)(2,1)S(1)}, u32[]{:S(2)}, u32[]{:S(2)}) collective-permute-start(bf16[128,1792]{1,0:T(8,128)(2,1)S(1)} %shard_map.130), channel_id=1, source_target_pairs={{0,240},{1,241},{2,242},{3,243},{4,244},{5,245},{6,246},{7,247},{8... | collective-permute-start | bytes 1376264 | tf_op jit(solution)/shard_map/ppermute | solution.py:187
  171.6 1.6 copy-start.6
  186.7 36.2 %all-to-all-start.5 = ((bf16[8,48,3584]{2,1,0:T(8,128)(2,1)}), bf16[8,48,3584]{2,1,0:T(8,128)(2,1)}, u32[]{:S(2)}, u32[]{:S(2)}) async-start(bf16[8,48,3584]{2,1,0:T(8,128)(2,1)} %bitcast.73), calls=%async_computation.5 | async-start | bytes 5505024 | tf_op jit(solution)/shard_map/all_to_all | solution.py:227
  191.2 15.6 %copy-start.2 = (bf16[208,1792]{1,0:T(8,128)(2,1)S(1)}, bf16[208,1792]{1,0:T(8,128)(2,1)}, u32[]{:S(2)}) copy-start(bf16[208,1792]{1,0:T(8,128)(2,1)} %copy-done) | copy-start | bytes 2236420
  198.1 8.7 %collective-permute-start.13 = (bf16[384,512]{1,0:T(8,128)(2,1)}, bf16[384,512]{1,0:T(8,128)(2,1)S(1)}, u32[]{:S(2)}, u32[]{:S(2)}) collective-permute-start(bf16[384,512]{1,0:T(8,128)(2,1)} %shard_map.132.own_ref), channel_id=1, source_target_pairs={{0,1},{1,0},{2,3},{3,2},{4,5},{5,4},{6,7},{7,6},{8,9},{9,8},{10,11... | collective-permute-start | bytes 1179656 | tf_op jit(solution)/shard_map/ppermute | solution.py:176
  206.8 1.0 copy-start.17
  209.7 1.1 copy-start.9
  222.9 23.6 %all-to-all-start.6 = ((bf16[8,48,1792]{2,1,0:T(8,128)(2,1)}), bf16[8,48,1792]{2,1,0:T(8,128)(2,1)}, u32[]{:S(2)}, u32[]{:S(2)}) async-start(bf16[8,48,1792]{2,1,0:T(8,128)(2,1)} %bitcast.77), calls=%async_computation.6 | async-start | bytes 2752512 | tf_op jit(solution)/shard_map/all_to_all | solution.py:227
  227.5 15.0 %copy-start.3 = (bf16[208,1792]{1,0:T(8,128)(2,1)S(1)}, bf16[208,1792]{1,0:T(8,128)(2,1)}, u32[]{:S(2)}) copy-start(bf16[208,1792]{1,0:T(8,128)(2,1)} %copy-done) | copy-start | bytes 2236420
  234.4 8.1 %collective-permute-start.14 = (bf16[384,512]{1,0:T(8,128)(2,1)}, bf16[384,512]{1,0:T(8,128)(2,1)S(1)}, u32[]{:S(2)}, u32[]{:S(2)}) collective-permute-start(bf16[384,512]{1,0:T(8,128)(2,1)} %shard_map.134.own_ref), channel_id=1, source_target_pairs={{0,1},{1,0},{2,3},{3,2},{4,5},{5,4},{6,7},{7,6},{8,9},{9,8},{10,11... | collective-permute-start | bytes 1179656 | tf_op jit(solution)/shard_map/ppermute | solution.py:176
  242.5 1.0 copy-start.15
  245.4 1.1 copy-start.7
  246.5 6.1 %copy-start.13 = (bf16[128,1792]{1,0:T(8,128)(2,1)S(1)}, bf16[128,1792]{1,0:T(8,128)(2,1)}, u32[]{:S(2)}) copy-start(bf16[128,1792]{1,0:T(8,128)(2,1)} %copy-done.12) | copy-start | bytes 1376260
  246.5 23.7 %all-to-all-start.7 = ((bf16[8,48,1792]{2,1,0:T(8,128)(2,1)}), bf16[8,48,1792]{2,1,0:T(8,128)(2,1)S(1)}, u32[]{:S(2)}, u32[]{:S(2)}) async-start(bf16[8,48,1792]{2,1,0:T(8,128)(2,1)} %bitcast.74), calls=%async_computation.7 | async-start | bytes 2752512 | tf_op jit(solution)/shard_map/all_to_all | solution.py:227
  254.5 12.0 %collective-permute-start.15 = (bf16[64,1792]{1,0:T(8,128)(2,1)S(1)}, bf16[64,1792]{1,0:T(8,128)(2,1)S(1)}, u32[]{:S(2)}, u32[]{:S(2)}) collective-permute-start(bf16[64,1792]{1,0:T(8,128)(2,1)S(1)} %get-tuple-element.82), channel_id=1, source_target_pairs={{0,16},{1,17},{2,18},{3,19},{4,20},{5,21},{6,22},{7,23},{8,24},{9,... | collective-permute-start | bytes 688136 | tf_op jit(solution)/shard_map/ppermute | solution.py:187
  263.6 6.6 %collective-permute-start.16 = (bf16[64,1792]{1,0:T(8,128)(2,1)S(1)}, bf16[64,1792]{1,0:T(8,128)(2,1)S(1)}, u32[]{:S(2)}, u32[]{:S(2)}) collective-permute-start(bf16[64,1792]{1,0:T(8,128)(2,1)S(1)} %get-tuple-element.83), channel_id=1, source_target_pairs={{0,17},{1,16},{2,19},{3,18},{4,21},{5,20},{6,23},{7,22},{8,25},{9,... | collective-permute-start | bytes 688136 | tf_op jit(solution)/shard_map/ppermute | solution.py:187
  270.8 12.2 %collective-permute-start.17 = (bf16[64,1792]{1,0:T(8,128)(2,1)S(1)}, bf16[64,1792]{1,0:T(8,128)(2,1)S(1)}, u32[]{:S(2)}, u32[]{:S(2)}) collective-permute-start(bf16[64,1792]{1,0:T(8,128)(2,1)S(1)} %get-tuple-element.78), channel_id=1, source_target_pairs={{0,240},{1,241},{2,242},{3,243},{4,244},{5,245},{6,246},{7,247},{8... | collective-permute-start | bytes 688136 | tf_op jit(solution)/shard_map/ppermute | solution.py:187
  273.1 15.1 %collective-permute-start.18 = (bf16[64,1792]{1,0:T(8,128)(2,1)S(1)}, bf16[64,1792]{1,0:T(8,128)(2,1)S(1)}, u32[]{:S(2)}, u32[]{:S(2)}) collective-permute-start(bf16[64,1792]{1,0:T(8,128)(2,1)S(1)} %get-tuple-element.79), channel_id=1, source_target_pairs={{0,241},{1,240},{2,243},{3,242},{4,245},{5,244},{6,247},{7,246},{8... | collective-permute-start | bytes 688136 | tf_op jit(solution)/shard_map/ppermute | solution.py:187
  (1 other events, 0.8 us)
